TPU v7x, 32 devices: a whole 2x2x4 slice. The times are simulated.
32 devices in a mesh: dp: 8 (over z, x), seq: 4 (over y, core).
Axes of the slice: x: 2, y: 2, z: 4, core: 2. Of those that a mesh axis runs over, the one named last changes fastest.
Arguments:
- tokens: bfloat16 [4096, 1152], P(('dp', 'seq')), may hold values from -6 to 6
- gain: float32 [1152], replicated, may hold values from 0.5 to 1.5
- w_qkv: bfloat16 [1152, 3456], replicated, may hold values from -0.1875 to 0.1875
- w_out: bfloat16 [1152, 1152], replicated, may hold values from -0.1875 to 0.1875
- dest: int32 [4096, 1], P(('dp', 'seq')), may hold values from 0 to 7; in each aligned block of 128 rows (0 to 127, 128 to 255, ...) at most 32 rows name the same one
- track: int32 [4096], P(('dp', 'seq')), may hold values from 0 to 3
- cotangent: bfloat16 [4096, 1152], P(('dp', 'seq')), may hold values from -6 to 6
Outputs:
- output: bfloat16 [4096, 1152], P(('dp', 'seq'))
- grad_tokens: bfloat16 [4096, 1152], P(('dp', 'seq'))
Inputs may be any that keep to these rules, and one draw needn't show every extreme that they name: `dest`: among the 128 tokens of one device, at most 32 name any one group, a bound that some block reaches.
All inputs are finite; a program needn't handle non-finite values.
Results may differ from a plain program's by a relative error of at most 0.0051.
Values may be sent and summed in bfloat16 or wider, within the bound.
A program may use at most 128 MiB of HBM per device.

v0:
```python
import jax
import jax.numpy as jnp
from jax import lax
from jax.sharding import PartitionSpec as P

HEADS = 16
HEAD = 72


def normalize(rows, gain):
    mean = jnp.mean(rows, axis=1, keepdims=True)
    centred = rows - mean
    var = jnp.mean(centred * centred, axis=1, keepdims=True)
    return centred * lax.rsqrt(var + 1e-06) * gain[None, :]


def masked_scores(query, keys, qtrack, ktrack):
    scores = jnp.einsum("qhe,khe->hqk", query, keys, preferred_element_type=jnp.float32)
    scores = scores * HEAD ** (-0.5)
    match = qtrack[:, None] == ktrack[None, :]
    return jnp.where(match[None], scores, -1e30)


def attend(query, keys, values, qtrack, ktrack):
    scores = masked_scores(query, keys, qtrack, ktrack)
    top = jnp.max(scores, axis=2, keepdims=True)
    expo = jnp.exp(scores - top)
    total = jnp.sum(expo, axis=2, keepdims=True)
    weights = (expo / total).astype(jnp.bfloat16)
    result = jnp.einsum("hqk,khe->qhe", weights, values, preferred_element_type=jnp.float32)
    return (result.astype(jnp.bfloat16), (top + jnp.log(total))[:, :, 0])


def attend_back(query, keys, values, result, grad_res, lse, qtrack, ktrack):
    scores = masked_scores(query, keys, qtrack, ktrack)
    prob = jnp.exp(scores - lse[:, :, None])
    weights = prob.astype(jnp.bfloat16)
    dprob = jnp.einsum("qhe,khe->hqk", grad_res, values, preferred_element_type=jnp.float32)
    delta = jnp.einsum("qhe,qhe->hq", grad_res, result, preferred_element_type=jnp.float32)
    dscore = (prob * (dprob - delta[:, :, None])).astype(jnp.bfloat16)
    scale = HEAD ** (-0.5)
    grad_q = jnp.einsum("hqk,khe->qhe", dscore, keys, preferred_element_type=jnp.float32) * scale
    grad_k = jnp.einsum("hqk,qhe->khe", dscore, query, preferred_element_type=jnp.float32) * scale
    grad_v = jnp.einsum("hqk,qhe->khe", weights, grad_res, preferred_element_type=jnp.float32)
    return (grad_q, grad_k, grad_v)


def local(tokens, gain, w_qkv, w_out, dest, track, cotangent):
    count = tokens.shape[0]
    groups = lax.axis_size("dp")
    capacity = 2 * count // groups
    slots = groups * capacity
    clip_group = dest[:, 0]
    onehot = (clip_group[:, None] == jnp.arange(groups, dtype=jnp.int32)[None, :]).astype(jnp.int32)
    rank = jnp.sum(jnp.cumsum(onehot, axis=0) * onehot, axis=1) - 1
    position = clip_group * capacity + rank
    placing = position[None, :] == jnp.arange(slots, dtype=jnp.int32)[:, None]
    place_b = placing.astype(jnp.bfloat16)
    place_back = place_b.T
    send_track = jnp.sum(placing.astype(jnp.int32) * (track + 1)[None, :], axis=1) - 1
    rows_f = tokens.astype(jnp.float32)
    normed, ln_back = jax.vjp(lambda value: normalize(value, gain), rows_f)
    qkv = jnp.dot(normed.astype(jnp.bfloat16), w_qkv, preferred_element_type=jnp.float32).astype(
        jnp.bfloat16
    )
    sent = jnp.dot(place_b, qkv, preferred_element_type=jnp.float32).astype(jnp.bfloat16)
    received, recv_track = (
        lax.all_to_all(sent, "dp", split_axis=0, concat_axis=0, tiled=True),
        lax.all_to_all(send_track, "dp", split_axis=0, concat_axis=0, tiled=True),
    )
    all_track = lax.all_gather(recv_track, "seq", axis=0, tiled=True)
    split = received.reshape(slots, 3, HEADS, HEAD)
    headwise = lax.all_to_all(split, "seq", split_axis=2, concat_axis=0, tiled=True)
    query, keys, values = (headwise[:, 0], headwise[:, 1], headwise[:, 2])
    result, lse = attend(query, keys, values, all_track, all_track)
    attended = lax.all_to_all(result, "seq", split_axis=0, concat_axis=1, tiled=True)
    back = lax.all_to_all(
        attended.reshape(slots, HEADS * HEAD), "dp", split_axis=0, concat_axis=0, tiled=True
    )
    att_rows = jnp.dot(place_back, back, preferred_element_type=jnp.float32).astype(jnp.bfloat16)
    output = (rows_f + jnp.dot(att_rows, w_out, preferred_element_type=jnp.float32)).astype(
        jnp.bfloat16
    )
    grad_att = lax.dot_general(
        cotangent, w_out, (((1,), (1,)), ((), ())), preferred_element_type=jnp.float32
    ).astype(jnp.bfloat16)
    grad_sent = jnp.dot(place_b, grad_att, preferred_element_type=jnp.float32).astype(jnp.bfloat16)
    grad_recv = lax.all_to_all(grad_sent, "dp", split_axis=0, concat_axis=0, tiled=True).reshape(
        slots, HEADS, HEAD
    )
    grad_heads = lax.all_to_all(grad_recv, "seq", split_axis=1, concat_axis=0, tiled=True)
    grad_q, grad_k, grad_v = attend_back(
        query, keys, values, result, grad_heads, lse, all_track, all_track
    )
    stacked = jnp.stack((grad_q, grad_k, grad_v), axis=1).astype(jnp.bfloat16)
    grad_slots = lax.all_to_all(stacked, "seq", split_axis=0, concat_axis=2, tiled=True)
    grad_home = lax.all_to_all(
        grad_slots.reshape(slots, 3 * HEADS * HEAD), "dp", split_axis=0, concat_axis=0, tiled=True
    )
    query_key_value_gradient = jnp.dot(
        place_back, grad_home, preferred_element_type=jnp.float32
    ).astype(jnp.bfloat16)
    grad_normed = lax.dot_general(
        query_key_value_gradient,
        w_qkv,
        (((1,), (1,)), ((), ())),
        preferred_element_type=jnp.float32,
    )
    grad_tokens = (cotangent.astype(jnp.float32) + ln_back(grad_normed)[0]).astype(jnp.bfloat16)
    return (output, grad_tokens)


def solution(mesh):
    return jax.shard_map(
        local,
        mesh=mesh,
        in_specs=(
            P(("dp", "seq"), None),
            P(),
            P(),
            P(),
            P(("dp", "seq"), None),
            P(("dp", "seq")),
            P(("dp", "seq"), None),
        ),
        out_specs=(P(("dp", "seq"), None), P(("dp", "seq"), None)),
        check_vma=False,
    )
```

profile of v0, /device:TPU:0, one launch (start us, length us, event | category | flops | bytes accessed | tf_op | source)
XLA Modules:
  0.0 321.3 jit_solution(11575852097836266539)
XLA Ops:
  0.7 0.9 fusion.41
  1.7 0.8 select_reduce_fusion.1
  2.6 0.7 add_add_fusion.1
  3.4 0.7 sub.45
  4.0 7.3 %all-to-all-start.2 = ((s32[8,32,1]{1,2,0:T(1,128)}), s32[8,32,1]{1,2,0:T(1,128)S(1)}, u32[]{:S(2)}, u32[]{:S(2)}) async-start(s32[8,32,1]{1,2,0:T(1,128)} %bitcast.8), calls=%async_computation.2 | async-start | bytes 8192 | tf_op jit(solution)/shard_map/all_to_all | solution.py:69
  11.3 3.0 convolution_convert_fusion.3
  14.9 2.8 all-to-all-done.2
  17.7 3.5 %all-to-all-start.5 = ((bf16[8,32,1152]{2,1,0:T(8,128)(2,1)}), bf16[8,32,1152]{2,1,0:T(8,128)(2,1)S(1)}, u32[]{:S(2)}, u32[]{:S(2)}) async-start(bf16[8,32,1152]{2,1,0:T(8,128)(2,1)} %bitcast.82), calls=%async_computation.5 | async-start | bytes 1179648 | tf_op jit(solution)/shard_map/all_to_all | solution.py:88
  23.8 6.4 %convolution_convert_fusion = bf16[256,3456]{1,0:T(8,128)(2,1)} fusion(bf16[1152,3456]{1,0:T(8,128)(2,1)} %param.9, bf16[128,1152]{1,0:T(8,128)(2,1)S(1)} %copy-done.2, f32[1152]{0:T(1024)S(1)} %copy-done.5, f32[128]{0:T(128)} %fusion.42, f32[128]{0:T(128)} %copy-done.10, s32[128]{0:T(128)S(1)} %get-tuple-element.8), kind=kOutput, calls=%fused_computation.10 | convolution fusion | flops 1247805440 | bytes 10033152 | tf_op jit(solution)/shard_map/dot_general | solution.py:66
  30.1 6.1 %all-to-all-done.5 = bf16[8,32,1152]{2,1,0:T(8,128)(2,1)S(1)} async-done(((bf16[8,32,1152]{2,1,0:T(8,128)(2,1)}), bf16[8,32,1152]{2,1,0:T(8,128)(2,1)S(1)}, u32[]{:S(2)}, u32[]{:S(2)}) %all-to-all-start.5) | async-done | bytes 589856 | tf_op jit(solution)/shard_map/all_to_all | solution.py:88
  36.3 4.3 %all-to-all-start = ((bf16[8,32,3456]{2,1,0:T(8,128)(2,1)}), bf16[8,32,3456]{2,1,0:T(8,128)(2,1)}, u32[]{:S(2)}, u32[]{:S(2)}) async-start(bf16[8,32,3456]{2,1,0:T(8,128)(2,1)} %bitcast.75), calls=%async_computation | async-start | bytes 3538944 | tf_op jit(solution)/shard_map/all_to_all | solution.py:68
  40.6 2.8 reshape.114
  43.4 2.3 copy.47
  45.8 35.1 %all-to-all-done = bf16[8,32,3456]{2,1,0:T(8,128)(2,1)} async-done(((bf16[8,32,3456]{2,1,0:T(8,128)(2,1)}), bf16[8,32,3456]{2,1,0:T(8,128)(2,1)}, u32[]{:S(2)}, u32[]{:S(2)}) %all-to-all-start) | async-done | bytes 1769504 | tf_op jit(solution)/shard_map/all_to_all | solution.py:68
  80.9 3.5 %all-to-all-start.6 = ((bf16[256,16,72]{0,2,1:T(8,128)(2,1)}), bf16[256,16,72]{0,2,1:T(8,128)(2,1)S(1)}, u32[]{:S(2)}, u32[]{:S(2)}) async-start(bf16[256,16,72]{0,2,1:T(8,128)(2,1)} %copy.47), calls=%async_computation.6 | async-start | bytes 1179648 | tf_op jit(solution)/shard_map/all_to_all | solution.py:91
  84.4 7.7 %reshape.113 = bf16[256,3,16,72]{3,2,1,0:T(8,128)(2,1)} reshape(bf16[8,32,3456]{2,1,0:T(8,128)(2,1)} %all-to-all-done) | data formatting | bytes 3538944 | tf_op jit(solution)/shard_map/reshape | solution.py:72
  92.1 4.8 %copy.40 = bf16[256,3,16,72]{0,3,1,2:T(8,128)(2,1)} copy(bf16[256,3,16,72]{3,2,1,0:T(8,128)(2,1)} %reshape.113) | data formatting | bytes 3538944 | tf_op jit(solution)/shard_map/reshape | solution.py:72
  96.8 4.4 %all-to-all-start.1 = ((bf16[256,3,16,72]{0,3,1,2:T(8,128)(2,1)}), bf16[256,3,16,72]{0,3,1,2:T(8,128)(2,1)}, u32[]{:S(2)}, u32[]{:S(2)}) async-start(bf16[256,3,16,72]{0,3,1,2:T(8,128)(2,1)} %copy.40), calls=%async_computation.1 | async-start | bytes 3538944 | tf_op jit(solution)/shard_map/all_to_all | solution.py:73
  102.5 21.8 %all-gather = s32[4,1,256]{2,1,0:T(1,128)S(1)} all-gather(s32[1,1,256]{2,1,0:T(1,128)S(1)} %reshape.115), channel_id=1, replica_groups=mesh['dp'=8,'seq'=4] {'seq'}, dimensions={0}, use_global_device_ids=true | all-gather | bytes 5120 | tf_op jit(solution)/shard_map/all_gather | solution.py:71
  124.3 1.6 broadcast_compare_fusion
  125.9 1.1 copy.68
  127.1 4.0 %copy.42 = bf16[4,256,3,4,72]{1,0,4,3,2:T(4,128)(2,1)} copy(bf16[4,256,3,4,72]{1,4,2,3,0:T(8,128)(2,1)} %bitcast.6) | data formatting | bytes 3538944 | tf_op jit(solution)/shard_map/all_to_all | solution.py:73
  131.1 4.2 %all_to_all.87 = bf16[1024,3,4,72]{0,3,2,1:T(8,128)(2,1)} reshape(bf16[4,256,3,4,72]{1,0,4,3,2:T(4,128)(2,1)} %copy.42) | data formatting | bytes 3538944 | tf_op jit(solution)/shard_map/all_to_all | solution.py:73
  135.3 10.6 %fusion.44 = (f32[4,1024]{1,0:T(4,128)S(1)}, f32[4,1024,1024]{1,2,0:T(8,128)}) fusion(bf16[1024,3,4,72]{0,3,2,1:T(8,128)(2,1)} %all_to_all.87, pred[1024,1024]{0,1:T(8,128)(4,1)} %broadcast_compare_fusion), kind=kOutput, calls=%fused_computation.71 | convolution fusion | flops 616558592 | bytes 19021824 | tf_op jit(solution)/shard_map/qhe,khe->hqk/dot_general | solution.py:18
  145.9 8.0 %fusion = f32[4,1024]{1,0:T(4,128)S(1)} fusion(f32[4,1024,1024]{1,2,0:T(8,128)} %get-tuple-element.3, f32[4,1024]{1,0:T(4,128)S(1)} %get-tuple-element.2), kind=kLoop, calls=%fused_computation.5 | loop fusion | flops 8384512 | bytes 16809984 | tf_op jit(solution)/shard_map/reduce_sum | solution.py:28
  153.9 10.4 %fusion.18 = (f32[4,1024]{1,0:T(4,128)}, bf16[4,72,1024]{2,1,0:T(8,128)(2,1)}) fusion(bf16[1024,4,72]{0,2,1:T(8,128)(2,1)S(1)} %bitcast.76, f32[4,1024,1024]{1,2,0:T(8,128)} %get-tuple-element.3, f32[4,1024]{1,0:T(4,128)S(1)} %fusion, f32[4,1024]{1,0:T(4,128)S(1)} %get-tuple-element.2, bf16[1024,3,4,72]{0,3,2,1:T(8,128)(2,1)} %all_to_all.87), kind=kOutput, calls=%fused_computation.32 | convolution fusion | flops 618033152 | bytes 18595840 | tf_op jit(solution)/shard_map/hqk,khe->qhe/dot_general | solution.py:30
  164.4 2.3 copy.45
  166.7 4.5 %all-to-all-start.3 = ((bf16[1024,4,72]{2,1,0:T(4,128)(2,1)}), bf16[1024,4,72]{2,1,0:T(4,128)(2,1)}, u32[]{:S(2)}, u32[]{:S(2)}) async-start(bf16[1024,4,72]{2,1,0:T(4,128)(2,1)} %copy.45), calls=%async_computation.3 | async-start | bytes 2097152 | tf_op jit(solution)/shard_map/all_to_all | solution.py:76
  171.2 8.6 %fusion.13 = bf16[1024,1,4,72]{0,3,2,1:T(8,128)(2,1)S(1)} fusion(bf16[1024,4,72]{0,2,1:T(8,128)(2,1)S(1)} %bitcast.77, f32[4,1024,1024]{1,2,0:T(8,128)} %get-tuple-element.3, f32[4,1024]{1,0:T(4,128)S(1)} %log_add_fusion), kind=kOutput, calls=%fused_computation.28 | convolution fusion | flops 612663296 | bytes 17973248 | tf_op jit(solution)/shard_map/hqk,qhe->khe/dot_general | solution.py:44
  179.8 9.6 %multiply_convert_fusion = bf16[4,1024,1024]{1,2,0:T(8,128)(2,1)} fusion(f32[4,1024,1024]{1,2,0:T(8,128)} %get-tuple-element.3, bf16[1024,4,72]{0,2,1:T(8,128)(2,1)S(1)} %bitcast.78, f32[4,1024]{1,0:T(4,128)S(1)} %copy-done.9, f32[4,1024]{1,0:T(4,128)S(1)} %log_add_fusion, bf16[1024,3,4,72]{0,3,2,1:T(8,128)(2,1)S(1)} %copy-done.3), kind=kOutput, calls=%fused_computation | convolution fusion | flops 620756992 | bytes 26378240 | tf_op jit(solution)/shard_map/qhe,khe->hqk/dot_general | solution.py:38
  189.4 6.2 %fusion.16 = bf16[1024,1,4,72]{0,3,2,1:T(8,128)(2,1)S(1)} fusion(bf16[4,1024,1024]{1,2,0:T(8,128)(2,1)} %multiply_convert_fusion, bf16[1024,3,4,72]{0,3,2,1:T(8,128)(2,1)S(1)} %copy-done.3), kind=kOutput, calls=%fused_computation.29 | convolution fusion | flops 604569600 | bytes 9568256 | tf_op jit(solution)/shard_map/hqk,qhe->khe/dot_general | solution.py:43
  195.6 1.6 fusion.17
  197.3 1.4 pad_maximum_fusion
  198.7 5.6 %copy.53 = bf16[1024,3,4,72]{3,2,1,0:T(4,128)(2,1)} copy(bf16[1024,3,4,72]{0,3,2,1:T(8,128)(2,1)} %pad_maximum_fusion) | data formatting | bytes 3538944 | tf_op jit(solution)/shard_map/stack | solution.py:95
  204.3 4.6 %all-to-all-start.7 = ((bf16[1024,3,4,72]{3,2,1,0:T(4,128)(2,1)}), bf16[1024,3,4,72]{3,2,1,0:T(4,128)(2,1)}, u32[]{:S(2)}, u32[]{:S(2)}) async-start(bf16[1024,3,4,72]{3,2,1,0:T(4,128)(2,1)} %copy.53), calls=%async_computation.7 | async-start | bytes 6291456 | tf_op jit(solution)/shard_map/all_to_all | solution.py:96
  208.9 2.6 copy.72
  211.5 3.8 %all_to_all.93 = bf16[8,32,1152]{2,1,0:T(8,128)(2,1)} reshape(bf16[256,4,4,72]{3,2,1,0:T(4,128)(2,1)} %bitcast.79) | data formatting | bytes 1179648 | tf_op jit(solution)/shard_map/all_to_all | solution.py:77
  215.3 30.6 %all-to-all-done.7 = bf16[1024,3,4,72]{3,2,1,0:T(4,128)(2,1)} async-done(((bf16[1024,3,4,72]{3,2,1,0:T(4,128)(2,1)}), bf16[1024,3,4,72]{3,2,1,0:T(4,128)(2,1)}, u32[]{:S(2)}, u32[]{:S(2)}) %all-to-all-start.7) | async-done | bytes 1769504 | tf_op jit(solution)/shard_map/all_to_all | solution.py:96
  245.9 3.8 %all-to-all-start.4 = ((bf16[8,32,1152]{2,1,0:T(8,128)(2,1)}), bf16[8,32,1152]{2,1,0:T(8,128)(2,1)S(1)}, u32[]{:S(2)}, u32[]{:S(2)}) async-start(bf16[8,32,1152]{2,1,0:T(8,128)(2,1)} %all_to_all.93), calls=%async_computation.4 | async-start | bytes 1179648 | tf_op jit(solution)/shard_map/all_to_all | solution.py:77
  249.7 4.6 %copy.71 = bf16[4,256,3,4,72]{4,3,0,2,1:T(4,128)(2,1)} copy(bf16[4,256,3,4,72]{4,3,2,1,0:T(4,128)(2,1)} %bitcast.26) | data formatting | bytes 3538944 | tf_op jit(solution)/shard_map/all_to_all | solution.py:96
  254.3 8.3 %all_to_all.105 = bf16[8,32,3456]{2,1,0:T(8,128)(2,1)} reshape(bf16[256,3,4,4,72]{4,3,2,1,0:T(4,128)(2,1)} %bitcast.74) | data formatting | bytes 3538944 | tf_op jit(solution)/shard_map/all_to_all | solution.py:97
  262.7 2.7 all-to-all-done.4
  265.4 4.3 %all-to-all-start.8 = ((bf16[8,32,3456]{2,1,0:T(8,128)(2,1)}), bf16[8,32,3456]{2,1,0:T(8,128)(2,1)}, u32[]{:S(2)}, u32[]{:S(2)}) async-start(bf16[8,32,3456]{2,1,0:T(8,128)(2,1)} %all_to_all.105), calls=%async_computation.8 | async-start | bytes 3538944 | tf_op jit(solution)/shard_map/all_to_all | solution.py:97
  269.7 1.5 fusion.6
  271.2 39.3 %all-to-all-done.8 = bf16[8,32,3456]{2,1,0:T(8,128)(2,1)} async-done(((bf16[8,32,3456]{2,1,0:T(8,128)(2,1)}), bf16[8,32,3456]{2,1,0:T(8,128)(2,1)}, u32[]{:S(2)}, u32[]{:S(2)}) %all-to-all-start.8) | async-done | bytes 1769504 | tf_op jit(solution)/shard_map/all_to_all | solution.py:97
  310.5 7.2 %fusion.26 = (f32[128]{0:T(128)}, f32[128,1152]{1,0:T(8,128)S(1)}) fusion(bf16[128,1152]{1,0:T(8,128)(2,1)S(1)} %copy-done.2, f32[128]{0:T(128)S(1)} %copy-done.11, f32[1152]{0:T(1024)S(1)} %copy-done.6, bf16[1152,3456]{1,0:T(8,128)(2,1)} %param.9, bf16[256,3456]{1,0:T(8,128)(2,1)} %bitcast.28, s32[128]{0:T(128)S(1)} %copy-done.8), kind=kOutput, calls=%fused_computation.44 | convolution fusion | flops 1246920576 | bytes 10622976 | tf_op jit(solution)/shard_map/dot_general | solution.py:103
  318.4 0.9 fusion.43
  319.3 2.0 add_convert_fusion
  (42 shorter events, 5.4 us)
Async XLA Ops:
  0.6 10.7 %copy-start = (bf16[1152,1152]{1,0:T(8,128)(2,1)S(1)}, bf16[1152,1152]{1,0:T(8,128)(2,1)}, u32[]{:S(2)}) copy-start(bf16[1152,1152]{1,0:T(8,128)(2,1)} %param.10) | copy-start | bytes 7962628
  0.6 13.6 %copy-start.2 = (bf16[128,1152]{1,0:T(8,128)(2,1)S(1)}, bf16[128,1152]{1,0:T(8,128)(2,1)}, u32[]{:S(2)}) copy-start(bf16[128,1152]{1,0:T(8,128)(2,1)} %param.7) | copy-start | bytes 884740
  0.7 23.1 %copy-start.5 = (f32[1152]{0:T(1024)S(1)}, f32[1152]{0:T(1024)}, u32[]{:S(2)}) copy-start(f32[1152]{0:T(1024)} %param.8) | copy-start | bytes 13828
  3.2 26.9 %copy-start.7 = (s32[128]{0:T(128)}, s32[128]{0:T(128)S(1)}, u32[]{:S(2)}) copy-start(s32[128]{0:T(128)S(1)} %get-tuple-element.8) | copy-start | bytes 1540
  4.0 13.6 %all-to-all-start.2 = ((s32[8,32,1]{1,2,0:T(1,128)}), s32[8,32,1]{1,2,0:T(1,128)S(1)}, u32[]{:S(2)}, u32[]{:S(2)}) async-start(s32[8,32,1]{1,2,0:T(1,128)} %bitcast.8), calls=%async_computation.2 | async-start | bytes 8192 | tf_op jit(solution)/shard_map/all_to_all | solution.py:69
  17.7 18.6 %all-to-all-start.5 = ((bf16[8,32,1152]{2,1,0:T(8,128)(2,1)}), bf16[8,32,1152]{2,1,0:T(8,128)(2,1)S(1)}, u32[]{:S(2)}, u32[]{:S(2)}) async-start(bf16[8,32,1152]{2,1,0:T(8,128)(2,1)} %bitcast.82), calls=%async_computation.5 | async-start | bytes 1179648 | tf_op jit(solution)/shard_map/all_to_all | solution.py:88
  21.9 0.5 copy-start.10
  22.7 0.5 copy-start.12
  36.3 44.6 %all-to-all-start = ((bf16[8,32,3456]{2,1,0:T(8,128)(2,1)}), bf16[8,32,3456]{2,1,0:T(8,128)(2,1)}, u32[]{:S(2)}, u32[]{:S(2)}) async-start(bf16[8,32,3456]{2,1,0:T(8,128)(2,1)} %bitcast.75), calls=%async_computation | async-start | bytes 3538944 | tf_op jit(solution)/shard_map/all_to_all | solution.py:68
  80.9 15.9 %all-to-all-start.6 = ((bf16[256,16,72]{0,2,1:T(8,128)(2,1)}), bf16[256,16,72]{0,2,1:T(8,128)(2,1)S(1)}, u32[]{:S(2)}, u32[]{:S(2)}) async-start(bf16[256,16,72]{0,2,1:T(8,128)(2,1)} %copy.47), calls=%async_computation.6 | async-start | bytes 1179648 | tf_op jit(solution)/shard_map/all_to_all | solution.py:91
  96.8 29.1 %copy-start.4 = (bf16[256,16,72]{0,2,1:T(8,128)(2,1)}, bf16[256,16,72]{0,2,1:T(8,128)(2,1)S(1)}, u32[]{:S(2)}) copy-start(bf16[256,16,72]{0,2,1:T(8,128)(2,1)S(1)} %all-to-all-done.6) | copy-start | bytes 1769476
  96.8 30.2 %all-to-all-start.1 = ((bf16[256,3,16,72]{0,3,1,2:T(8,128)(2,1)}), bf16[256,3,16,72]{0,3,1,2:T(8,128)(2,1)}, u32[]{:S(2)}, u32[]{:S(2)}) async-start(bf16[256,3,16,72]{0,3,1,2:T(8,128)(2,1)} %copy.40), calls=%async_computation.1 | async-start | bytes 3538944 | tf_op jit(solution)/shard_map/all_to_all | solution.py:73
  166.7 37.6 %all-to-all-start.3 = ((bf16[1024,4,72]{2,1,0:T(4,128)(2,1)}), bf16[1024,4,72]{2,1,0:T(4,128)(2,1)}, u32[]{:S(2)}, u32[]{:S(2)}) async-start(bf16[1024,4,72]{2,1,0:T(4,128)(2,1)} %copy.45), calls=%async_computation.3 | async-start | bytes 2097152 | tf_op jit(solution)/shard_map/all_to_all | solution.py:76
  171.2 8.6 %copy-start.3 = (bf16[1024,3,4,72]{0,3,2,1:T(8,128)(2,1)S(1)}, bf16[1024,3,4,72]{0,3,2,1:T(8,128)(2,1)}, u32[]{:S(2)}) copy-start(bf16[1024,3,4,72]{0,3,2,1:T(8,128)(2,1)} %all_to_all.87) | copy-start | bytes 5308420
  171.2 8.6 %copy-start.9 = (f32[4,1024]{1,0:T(4,128)S(1)}, f32[4,1024]{1,0:T(4,128)}, u32[]{:S(2)}) copy-start(f32[4,1024]{1,0:T(4,128)} %get-tuple-element.4) | copy-start | bytes 49156
  189.4 6.2 %copy-start.1 = (bf16[4,1024,1024]{1,2,0:T(8,128)(2,1)S(1)}, bf16[4,1024,1024]{1,2,0:T(8,128)(2,1)}, u32[]{:S(2)}) copy-start(bf16[4,1024,1024]{1,2,0:T(8,128)(2,1)} %multiply_convert_fusion) | copy-start | bytes 25165828
  204.3 41.6 %all-to-all-start.7 = ((bf16[1024,3,4,72]{3,2,1,0:T(4,128)(2,1)}), bf16[1024,3,4,72]{3,2,1,0:T(4,128)(2,1)}, u32[]{:S(2)}, u32[]{:S(2)}) async-start(bf16[1024,3,4,72]{3,2,1,0:T(4,128)(2,1)} %copy.53), calls=%async_computation.7 | async-start | bytes 6291456 | tf_op jit(solution)/shard_map/all_to_all | solution.py:96
  245.9 19.4 %all-to-all-start.4 = ((bf16[8,32,1152]{2,1,0:T(8,128)(2,1)}), bf16[8,32,1152]{2,1,0:T(8,128)(2,1)S(1)}, u32[]{:S(2)}, u32[]{:S(2)}) async-start(bf16[8,32,1152]{2,1,0:T(8,128)(2,1)} %all_to_all.93), calls=%async_computation.4 | async-start | bytes 1179648 | tf_op jit(solution)/shard_map/all_to_all | solution.py:77
  254.3 15.3 %copy-start.8 = (s32[128]{0:T(128)S(1)}, s32[128]{0:T(128)}, u32[]{:S(2)}) copy-start(s32[128]{0:T(128)} %copy-done.7) | copy-start | bytes 1540
  262.7 47.8 %copy-start.6 = (f32[1152]{0:T(1024)S(1)}, f32[1152]{0:T(1024)}, u32[]{:S(2)}) copy-start(f32[1152]{0:T(1024)} %param.8) | copy-start | bytes 13828
  262.7 47.8 %copy-start.11 = (f32[128]{0:T(128)S(1)}, f32[128]{0:T(128)}, u32[]{:S(2)}) copy-start(f32[128]{0:T(128)} %copy-done.10) | copy-start | bytes 1540
  265.4 45.1 %all-to-all-start.8 = ((bf16[8,32,3456]{2,1,0:T(8,128)(2,1)}), bf16[8,32,3456]{2,1,0:T(8,128)(2,1)}, u32[]{:S(2)}, u32[]{:S(2)}) async-start(bf16[8,32,3456]{2,1,0:T(8,128)(2,1)} %all_to_all.105), calls=%async_computation.8 | async-start | bytes 3538944 | tf_op jit(solution)/shard_map/all_to_all | solution.py:97
where the time goes:
time: 323 us; the launch traced here: 321 us
  waiting for transfers between devices  117 us (36%)
  matrix products  65.1 us (20%)
  local copies, waits for them, and re-layouts  56.5 us (17%)
  starting transfers between devices  40.2 us (12%)
  blocking collectives  21.8 us (7%)
  other arithmetic  20.1 us (6%)
    all_to_all x1, waiting for transfers between devices, local(): lax.all_to_all(grad_slots.reshape(slots, 3 * HEADS * HEAD), 'dp', split_a...  39.3 us
    all_to_all x1, waiting for transfers between devices, local(): lax.all_to_all(sent, 'dp', split_axis=0, concat_axis=0, tiled=True)  35.1 us
    all_to_all x1, waiting for transfers between devices, local(): lax.all_to_all(stacked, 'seq', split_axis=0, concat_axis=2, tiled=True)  30.6 us
    all_gather x1, blocking collectives, local(): all_track = lax.all_gather(recv_track, 'seq', axis=0, tiled=True)  21.8 us
    reshape x2, local copies, waits for them, and re-layouts, local(): split = received.reshape(slots, 3, HEADS, HEAD)  12.5 us
    dot_general x1, matrix products, masked_scores(): jnp.einsum('qhe,khe->hqk', query, keys, preferred_element_type=jnp.float32)  10.6 us
    dot_general x1, matrix products, attend(): jnp.einsum('hqk,khe->qhe', weights, values, preferred_element_type=jnp.fl...  10.4 us
    dot_general x1, matrix products, attend_back(): jnp.einsum('qhe,khe->hqk', grad_res, values, preferred_element_type=jnp.f...  9.64 us
  transfers between devices with their start and end apart: 9, of which 6 were waited for; matrix products, arithmetic and copies ran while one was open for 23% of the time, Pallas kernels for 0%

commit v1 on v0

v1 whole, which is shorter than its diff:
```python
import functools

import jax
import jax.numpy as jnp
from jax import lax
from jax.experimental import pallas as pl
from jax.experimental.pallas import tpu as pltpu
from jax.sharding import PartitionSpec as P

HEADS = 16
HEAD = 72
LANES = 128
SCALE = HEAD ** (-0.5)
MESH = pl.DeviceIdType.MESH
VMEM = pl.BlockSpec(memory_space=pltpu.VMEM)
BF = jnp.bfloat16
F32 = jnp.float32
NT = (((1,), (1,)), ((), ()))
TN = (((0,), (0,)), ((), ()))


def dot(a, b, dims=(((1,), (0,)), ((), ()))):
    return lax.dot_general(a, b, dims, preferred_element_type=F32)


def flip(index, mask):
    bit = 1
    out = index
    while bit <= mask:
        if mask & bit:
            out = out + bit * (1 - 2 * ((index // bit) % 2))
        bit *= 2
    return out


def greet(partners):
    barrier = pltpu.get_barrier_semaphore()
    for device in partners:
        pl.semaphore_signal(barrier, inc=1, device_id=device, device_id_type=MESH)
    pl.semaphore_wait(barrier, len(partners))


def partners_of(groups):
    me, part = lax.axis_index("dp"), lax.axis_index("seq")
    far = [(flip(me, o), part) for o in range(groups)]
    return far, (me, flip(part, 1)), (me, flip(part, 2)), me


def gather_kernel(groups, width, pay, wqkv, wout, qkv, gatt, tracks, held, s_dp, r_dp, s_y, r_y, s_c, r_c):
    far, sibling, across, me = partners_of(groups)
    greet(far[1:] + [sibling, across])
    cap = pay.shape[1]

    def remote(src, dst, send, recv, device):
        return pltpu.make_async_remote_copy(
            src_ref=src, dst_ref=dst, send_sem=send, recv_sem=recv, device_id=device, device_id_type=MESH
        )

    first = [
        remote(pay.at[far[o][0]], held.at[o, 0], s_dp.at[o], r_dp.at[o], far[o]) if o else None
        for o in range(groups)
    ]
    half = groups // 2
    for o in list(range(half, groups)) + list(range(1, half)):
        first[o].start()
    held[0, 0] = pay[me]
    to_y = [remote(held.at[o, 0], held.at[o, 2], s_y.at[o], r_y.at[o], across) for o in range(groups)]
    to_c = [remote(held.at[o, 0], held.at[o, 1], s_c.at[o, 0], r_c.at[o, 0], sibling) for o in range(groups)]
    to_d = [remote(held.at[o, 2], held.at[o, 3], s_c.at[o, 1], r_c.at[o, 1], sibling) for o in range(groups)]
    for step in range(groups + 2):
        if step < groups:
            if step:
                first[step].wait_recv()
            to_y[step].start()
            to_c[step].start()
        if 1 <= step <= groups:
            to_y[step - 1].wait_recv()
            to_d[step - 1].start()
        if step >= 2:
            o = step - 2
            to_c[o].wait_recv()
            to_d[o].wait_recv()
            block = held[o].reshape(4 * cap, held.shape[3])
            rows = pl.ds(o * 4 * cap, 4 * cap)
            qkv[rows, :] = dot(block[:, :width], wqkv[...]).astype(BF)
            gatt[rows, :] = dot(block[:, width : 2 * width], wout[...], NT).astype(BF)
            tracks[rows, :] = block[:, 2 * width :]
    for o in range(groups):
        if o:
            first[o].wait_send()
        to_y[o].wait_send()
        to_c[o].wait_send()
        to_d[o].wait_send()


def gather(pay, wqkv, wout, groups, width):
    cap, columns = pay.shape[1:]
    slots = groups * cap * 4
    sems = pltpu.SemaphoreType.DMA
    return pl.pallas_call(
        functools.partial(gather_kernel, groups, width),
        out_shape=(
            jax.ShapeDtypeStruct((slots, wqkv.shape[1]), BF),
            jax.ShapeDtypeStruct((slots, wout.shape[0]), BF),
            jax.ShapeDtypeStruct((slots, LANES), BF),
        ),
        in_specs=[VMEM] * 3,
        out_specs=(VMEM,) * 3,
        scratch_shapes=[
            pltpu.VMEM((groups, 4, cap, columns), BF),
            sems((groups,)), sems((groups,)), sems((groups,)), sems((groups,)),
            sems((groups, 2)), sems((groups, 2)),
        ],
        compiler_params=pltpu.CompilerParams(
            collective_id=0, has_side_effects=True, vmem_limit_bytes=48 * 2**20
        ),
    )(pay, wqkv, wout)


def scatter_kernel(groups, width, att, dqkv, wqkv, wout, out, part, near, total, passed, crossed, ready, s_dp, r_dp, s_y, r_y, s_c, r_c):
    far, sibling, across, me = partners_of(groups)
    greet(far[1:] + [sibling, across])
    cap = out.shape[1]

    def remote(src, dst, send, recv, device):
        return pltpu.make_async_remote_copy(
            src_ref=src, dst_ref=dst, send_sem=send, recv_sem=recv, device_id=device, device_id_type=MESH
        )

    to_c = [
        [remote(part.at[o, 2 * j + 1], near.at[o, j], s_c.at[o, j], r_c.at[o, j], sibling) for j in (0, 1)]
        for o in range(groups)
    ]
    to_y = [remote(passed.at[o], crossed.at[o], s_y.at[o], r_y.at[o], across) for o in range(groups)]
    home = [
        remote(ready.at[o], out.at[o], s_dp.at[o], r_dp.at[o], far[o]) if o else None
        for o in range(groups)
    ]
    half = groups // 2
    order = list(range(half, groups)) + list(range(1, half)) + [0]

    def compute(o):
        rows = pl.ds(o * 4 * cap, 4 * cap)
        part[o, :, :, :width] = dot(att[rows, :], wout[...]).astype(BF).reshape(4, cap, width)
        part[o, :, :, width:] = dot(dqkv[rows, :], wqkv[...], NT).astype(BF).reshape(4, cap, width)
        to_c[o][0].start()
        to_c[o][1].start()

    def middle(o):
        to_c[o][0].wait_recv()
        to_c[o][1].wait_recv()
        passed[o] = (part[o, 2].astype(F32) + near[o, 1].astype(F32)).astype(BF)
        to_y[o].start()
        total[o] = (part[o, 0].astype(F32) + near[o, 0].astype(F32)).astype(BF)

    def last(o):
        to_y[o].wait_recv()
        value = (total[o].astype(F32) + crossed[o].astype(F32)).astype(BF)
        if o:
            ready[o] = value
            home[o].start()
        else:
            out[0] = value

    for step in range(groups + 2):
        if step < groups:
            compute(order[step])
        if 1 <= step <= groups:
            middle(order[step - 1])
        if step >= 2:
            last(order[step - 2])
    for o in order:
        to_c[o][0].wait_send()
        to_c[o][1].wait_send()
        to_y[o].wait_send()
        if o:
            home[o].wait()


def scatter(att, dqkv, wqkv, wout, groups, width):
    slots = att.shape[0]
    cap = slots // (4 * groups)
    sems = pltpu.SemaphoreType.DMA
    one = pltpu.VMEM((groups, cap, 2 * width), BF)
    return pl.pallas_call(
        functools.partial(scatter_kernel, groups, width),
        out_shape=jax.ShapeDtypeStruct((groups, cap, 2 * width), BF),
        in_specs=[VMEM] * 4,
        out_specs=VMEM,
        scratch_shapes=[
            pltpu.VMEM((groups, 4, cap, 2 * width), BF),
            pltpu.VMEM((groups, 2, cap, 2 * width), BF),
            one, one, one, one,
            sems((groups,)), sems((groups,)), sems((groups,)), sems((groups,)),
            sems((groups, 2)), sems((groups, 2)),
        ],
        compiler_params=pltpu.CompilerParams(
            collective_id=1, has_side_effects=True, vmem_limit_bytes=56 * 2**20
        ),
    )(att, dqkv, wqkv, wout)


def attention_kernel(tiles, query, key, value, grad, tq, tk, att, dq, dk, dv, dk_t, dv_t):
    tile = pl.program_id(1)
    q, k, v, g = query[...], key[...], value[...], grad[...]
    scores = jnp.where(tq[...] == tk[...], dot(q, k, NT) * SCALE, -1e30)
    top = jnp.max(scores, axis=1, keepdims=True)
    expo = jnp.exp(scores - top)
    prob = expo * (1.0 / jnp.sum(expo, axis=1, keepdims=True))
    weights = prob.astype(BF)
    result = dot(weights, v).astype(BF)
    att[...] = result
    delta = jnp.sum(g.astype(F32) * result.astype(F32), axis=1, keepdims=True)
    dscore = (prob * (dot(g, v, NT) - delta)).astype(BF)
    dq[...] = (dot(dscore, k) * SCALE).astype(BF)

    @pl.when(tile == 0)
    def _():
        dk_t[...] = jnp.zeros_like(dk_t)
        dv_t[...] = jnp.zeros_like(dv_t)

    dk_t[...] += dot(q, dscore, TN)
    dv_t[...] += dot(g, weights, TN)

    @pl.when(tile == tiles - 1)
    def _():
        dk[...] = (dk_t[...].T * SCALE).astype(BF)
        dv[...] = dv_t[...].T.astype(BF)


def attention(qkv, gatt, track):
    slots = qkv.shape[0]
    heads = gatt.shape[1] // LANES
    rows = min(256, slots)
    tiles = slots // rows
    whole = lambda first: pl.BlockSpec((slots, LANES), lambda h, t: (0, first + h))
    part = pl.BlockSpec((rows, LANES), lambda h, t: (t, h))
    out = jax.ShapeDtypeStruct((slots, heads * LANES), BF)
    return pl.pallas_call(
        functools.partial(attention_kernel, tiles),
        grid=(heads, tiles),
        out_shape=(out,) * 4,
        in_specs=[
            part, whole(heads), whole(2 * heads), part,
            pl.BlockSpec((rows, 1), lambda h, t: (t, 0)),
            pl.BlockSpec((1, slots), lambda h, t: (0, 0)),
        ],
        out_specs=(part, part, whole(0), whole(0)),
        scratch_shapes=[pltpu.VMEM((LANES, slots), F32), pltpu.VMEM((LANES, slots), F32)],
        compiler_params=pltpu.CompilerParams(vmem_limit_bytes=48 * 2**20),
    )(qkv, qkv, qkv, gatt, track[:, None], track[None, :])


def normalize(rows, gain):
    mean = jnp.mean(rows, axis=1, keepdims=True)
    centred = rows - mean
    var = jnp.mean(centred * centred, axis=1, keepdims=True)
    return centred * lax.rsqrt(var + 1e-06) * gain[None, :]


def local(tokens, gain, w_qkv, w_out, dest, track, cotangent):
    count, width = tokens.shape
    groups, parts = lax.axis_size("dp"), lax.axis_size("seq")
    capacity = 2 * count // groups
    slots = groups * capacity
    heads = HEADS // parts
    me, part = lax.axis_index("dp"), lax.axis_index("seq")
    own = capacity % 16 == 0 and parts == 4

    clip_group = dest[:, 0]
    onehot = (clip_group[:, None] == jnp.arange(groups, dtype=jnp.int32)[None, :]).astype(jnp.int32)
    rank = jnp.sum(jnp.cumsum(onehot, axis=0) * onehot, axis=1) - 1
    slot_ids = jnp.arange(slots, dtype=jnp.int32)
    placing = (clip_group * capacity + rank)[None, :] == slot_ids[:, None]
    group_back = clip_group ^ me if own else clip_group
    placing_back = (group_back * capacity + rank)[:, None] == slot_ids[None, :]

    rows_f = tokens.astype(F32)
    normed, ln_back = jax.vjp(lambda value: normalize(value, gain), rows_f)
    marks = jnp.broadcast_to((track + 1).astype(BF)[:, None], (count, LANES))
    payload = jnp.concatenate([normed.astype(BF), cotangent, marks], axis=1)
    payload = dot(placing.astype(BF), payload).astype(BF).reshape(groups, capacity, -1)

    pad = LANES - HEAD
    mine = lax.dynamic_index_in_dim(w_qkv.reshape(width, 3, parts, heads, HEAD), part, 2, keepdims=False)
    mine = jnp.pad(mine, ((0, 0), (0, 0), (0, 0), (0, pad))).reshape(width, 3 * heads * LANES)
    mine_out = lax.dynamic_index_in_dim(w_out.reshape(parts, heads, HEAD, width), part, 0, keepdims=False)
    mine_out = jnp.pad(mine_out, ((0, 0), (0, pad), (0, 0))).reshape(heads * LANES, width)

    if own:
        qkv, gatt, marked = gather(payload, mine, mine_out, groups, width)
    else:
        moved = lax.all_to_all(payload.reshape(slots, -1), "dp", split_axis=0, concat_axis=0, tiled=True)
        moved = lax.all_gather(moved, "seq", axis=0, tiled=True)
        qkv = dot(moved[:, :width], mine).astype(BF)
        gatt = dot(moved[:, width : 2 * width], mine_out, NT).astype(BF)
        marked = moved[:, 2 * width :]

    att, dq, dk, dv = attention(qkv, gatt, marked[:, 0].astype(F32))
    dqkv = jnp.concatenate([dq, dk, dv], axis=1)

    if own:
        back = scatter(att, dqkv, mine, mine_out, groups, width)
    else:
        sums = jnp.concatenate([dot(att, mine_out), dot(dqkv, mine, NT)], axis=1).astype(BF)
        sums = lax.all_to_all(sums.reshape(parts, slots, -1), "seq", split_axis=0, concat_axis=0, tiled=True)
        sums = jnp.sum(sums.astype(F32), axis=0).astype(BF)
        back = lax.all_to_all(sums, "dp", split_axis=0, concat_axis=0, tiled=True)

    back = dot(placing_back.astype(BF), back.reshape(slots, 2 * width))
    output = (rows_f + back[:, :width]).astype(BF)
    grad_tokens = (cotangent.astype(F32) + ln_back(back[:, width:])[0]).astype(BF)
    return (output, grad_tokens)


def solution(mesh):
    return jax.shard_map(
        local,
        mesh=mesh,
        in_specs=(
            P(("dp", "seq"), None),
            P(),
            P(),
            P(),
            P(("dp", "seq"), None),
            P(("dp", "seq")),
            P(("dp", "seq"), None),
        ),
        out_specs=(P(("dp", "seq"), None), P(("dp", "seq"), None)),
        check_vma=False,
    )
```

time: 323 us -> 166 us (0.51)
  Pallas kernels: 0 us -> 122 us
  waiting for transfers between devices: 117 us -> 0 us
  matrix products: 65.1 us -> 3.3 us
  starting transfers between devices: 40.2 us -> 0 us
  local copies, waits for them, and re-layouts: 56.5 us -> 27.8 us
  blocking collectives: 21.8 us -> 0 us
  other arithmetic: 20.1 us -> 11.2 us
    pallas_call x0 -> x3, Pallas kernels: none -> 122 us  [the longest x1 49.5 us: scatter(): pl.pallas_call(functools.partial(scatter_kernel, groups, width), out_shap...]
    all_to_all x9 -> x0, waiting for transfers between devices: 117 us -> none  [the longest x1 39.3 us: local(): lax.all_to_all(grad_slots.reshape(slots, 3 * HEADS * HEAD), 'dp', split_a...]
    dot_general x10 -> x2, matrix products: 65.1 us -> 3.3 us  [dot(): return lax.dot_general(a, b, dims, preferred_element_type=F32)]
    all_to_all x9 -> x0, starting transfers between devices: 40.2 us -> none  [the longest x1 7.25 us: local(): lax.all_to_all(send_track, 'dp', split_axis=0, concat_axis=0, tiled=True)]
    all_to_all x8 -> x0, local copies, waits for them, and re-layouts: 29.2 us -> none  [the longest x1 8.31 us: local(): lax.all_to_all(grad_slots.reshape(slots, 3 * HEADS * HEAD), 'dp', split_a...]
    all_gather x1 -> x0, blocking collectives: 21.8 us -> none  [local(): all_track = lax.all_gather(recv_track, 'seq', axis=0, tiled=True)]
    unnamed x27 -> x15, local copies, waits for them, and re-layouts: 1.17 us -> 16.9 us
    reshape x4 -> x1, local copies, waits for them, and re-layouts: 17.6 us -> 5.74 us  [local(): jnp.pad(mine, ((0, 0), (0, 0), (0, 0), (0, pad)))]
  transfers between devices with their start and end apart: 9 -> 0, of which waited for: 6 -> 0; matrix products, arithmetic and copies ran while one was open for 23% -> 0% of each run, Pallas kernels for 0% -> 0%
where the time goes in v1:
time: 166 us
  Pallas kernels  122 us (73%)
  local copies, waits for them, and re-layouts  27.8 us (17%)
  other arithmetic  11.2 us (7%)
  matrix products  3.3 us (2%)
    pallas_call x1, Pallas kernels, scatter(): pl.pallas_call(functools.partial(scatter_kernel, groups, width), out_shap...  49.5 us
    pallas_call x1, Pallas kernels, gather(): pl.pallas_call(functools.partial(gather_kernel, groups, width), out_shape...  45.8 us
    pallas_call x1, Pallas kernels, attention(): pl.pallas_call(functools.partial(attention_kernel, tiles), grid=(heads, t...  27.2 us
    unnamed x15, local copies, waits for them, and re-layouts  16.9 us
    reshape x1, local copies, waits for them, and re-layouts, local(): jnp.pad(mine, ((0, 0), (0, 0), (0, 0), (0, pad)))  5.74 us

profile of v1, /device:TPU:0, one launch (start us, length us, event | category | flops | bytes accessed | tf_op | source)
XLA Modules:
  0.0 165.5 jit_solution(7288351403367485049)
XLA Ops:
  0.6 0.0 copy-start
  0.6 0.0 copy-start.5
  0.7 1.7 %copy-done = bf16[1152,1152]{1,0:T(8,128)(2,1)S(1)} copy-done((bf16[1152,1152]{1,0:T(8,128)(2,1)S(1)}, bf16[1152,1152]{1,0:T(8,128)(2,1)}, u32[]{:S(2)}) %copy-start) | copy-done | bytes 2654232
  2.4 0.7 add_convert_fusion.1
  3.0 1.1 convert_reduce_fusion
  4.1 1.2 fusion.9
  5.3 0.1 broadcast_in_dim.6
  5.4 0.7 fusion.18
  6.2 0.2 reduce_window_sum.11
  6.3 0.8 select_reduce_fusion
  7.2 0.7 fusion.19
  7.8 0.7 multiply_add_fusion.1
  8.5 1.2 fusion.11
  9.7 0.1 dynamic-slice_bitcast_fusion.1
  9.8 1.1 pad.9
  10.8 0.0 copy-done.5
  10.9 1.6 convolution_convert_fusion
  12.5 11.5 %copy.10 = bf16[1152,3456]{0,1:T(8,128)(2,1)} copy(bf16[1152,3456]{1,0:T(8,128)(2,1)} %param.9) | data formatting | bytes 15925248 | tf_op args[2]
  24.0 1.7 %dynamic-slice_bitcast_fusion = bf16[1152,3,4,72]{0,3,2,1:T(8,128)(2,1)S(1)} fusion(bf16[1152,3,4,4,72]{0,4,3,2,1:T(8,128)(2,1)} %bitcast.26, s32[]{:T(128)S(6)} %select_n.6), kind=kLoop, calls=%fused_computation.2 | loop fusion | bytes 3981316 | tf_op jit(solution)/shard_map/jit(dynamic_index_in_dim)/squeeze | solution.py:285
  25.7 2.3 %pad.8 = bf16[1152,3,4,128]{0,3,2,1:T(8,128)(2,1)} pad(bf16[1152,3,4,72]{0,3,2,1:T(8,128)(2,1)S(1)} %dynamic-slice_bitcast_fusion, bf16[]{:T(256)} %constant.42.clone.1), padding=0_0x0_0x0_0x0_56 | pad | bytes 5529602 | tf_op jit(solution)/shard_map/jit(_pad)/pad | solution.py:286
  28.0 5.7 %copy.12.wqkv = bf16[1152,1536]{1,0:T(8,128)(2,1)} copy(bf16[1152,1536]{0,1:T(8,128)(2,1)} %bitcast.25) | data formatting | bytes 7077888 | tf_op jit(solution)/shard_map/reshape | solution.py:286
  33.7 0.0 copy-start.1
  33.7 1.3 copy-done.1
  35.0 0.0 copy-start.2
  35.0 1.3 copy-done.2
  36.3 45.8 %shard_map.86 = (bf16[1024,1536]{1,0:T(8,128)(2,1)}, bf16[1024,512]{1,0:T(8,128)(2,1)S(1)}, bf16[1024,128]{1,0:T(8,128)(2,1)S(1)}) custom-call(bf16[8,32,2432]{2,1,0:T(8,128)(2,1)S(1)} %bitcast.23, bf16[1152,1536]{1,0:T(8,128)(2,1)} %copy.12.wqkv, bf16[512,1152]{1,0:T(8,128)(2,1)S(1)} %bitcast.22), custom_call_target="tpu_custom_call" | custom-call | tf_op jit(solution)/shard_map/pallas_call | solution.py:100
  82.0 0.1 fusion.15
  82.2 27.2 %shard_map.87 = (bf16[1024,512]{1,0:T(8,128)(2,1)S(1)}, bf16[1024,512]{1,0:T(8,128)(2,1)S(1)}, bf16[1024,512]{1,0:T(8,128)(2,1)S(1)}, bf16[1024,512]{1,0:T(8,128)(2,1)S(1)}) custom-call(bf16[1024,1536]{1,0:T(8,128)(2,1)} %get-tuple-element.9.query.key.value, bf16[1024,1536]{1,0:T(8,128)(2,1)} %get-tuple-element.9.query.key.value, ...), custom_call_target="tpu_custom_call" | custom-call | tf_op jit(solution)/shard_map/pallas_call | solution.py:239
  109.4 0.0 copy-start.3
  109.4 1.1 copy-done.3
  110.5 1.8 %pad_maximum_fusion.dqkv = bf16[1024,1536]{1,0:T(8,128)(2,1)} fusion(bf16[1024,512]{1,0:T(8,128)(2,1)S(1)} %get-tuple-element.15, bf16[1024,512]{1,0:T(8,128)(2,1)S(1)} %get-tuple-element.14, bf16[1024,512]{1,0:T(8,128)(2,1)S(1)} %get-tuple-element.13), kind=kLoop, calls=%fused_computation.1 | loop fusion | flops 9437184 | bytes 6291456 | tf_op jit(solution)/shard_map/concatenate | solution.py:300
  112.3 0.0 copy-start.6
  112.3 49.5 %shard_map.88 = bf16[8,32,2304]{2,1,0:T(8,128)(2,1)} custom-call(bf16[1024,512]{1,0:T(8,128)(2,1)} %copy-done.3, bf16[1024,1536]{1,0:T(8,128)(2,1)} %pad_maximum_fusion.dqkv, bf16[1152,1536]{1,0:T(8,128)(2,1)} %copy.12.wqkv, bf16[512,1152]{1,0:T(8,128)(2,1)} %bitcast.21), custom_call_target="tpu_custom_call" | custom-call | tf_op jit(solution)/shard_map/pallas_call | solution.py:185
  161.7 0.0 copy-start.4
  161.7 1.7 %fusion.14 = f32[128,2304]{1,0:T(8,128)S(1)} fusion(bf16[256,2304]{1,0:T(8,128)(2,1)} %bitcast.27, s32[128]{0:T(128)S(1)} %fusion.19), kind=kOutput, calls=%fused_computation.27 | convolution fusion | flops 151027712 | bytes 2359808 | tf_op jit(solution)/shard_map/dot_general | solution.py:23
  163.4 0.0 copy-done.6
  163.4 0.0 copy-done.4
  163.5 0.2 fusion.12
  163.7 0.9 fusion.22
  164.7 0.9 add_convert_fusion
  (5 shorter events, 0.1 us)
Async XLA Ops:
  0.6 1.8 %copy-start = (bf16[1152,1152]{1,0:T(8,128)(2,1)S(1)}, bf16[1152,1152]{1,0:T(8,128)(2,1)}, u32[]{:S(2)}) copy-start(bf16[1152,1152]{1,0:T(8,128)(2,1)} %param.10) | copy-start | bytes 7962628
  0.6 10.2 %copy-start.5 = (bf16[128,1152]{1,0:T(8,128)(2,1)S(1)}, bf16[128,1152]{1,0:T(8,128)(2,1)}, u32[]{:S(2)}) copy-start(bf16[128,1152]{1,0:T(8,128)(2,1)} %param.13) | copy-start | bytes 884740
  33.7 1.3 copy-start.1
  35.0 1.3 copy-start.2
  109.4 1.1 copy-start.3
  112.3 51.2 %copy-start.6 = (f32[1152]{0:T(1024)S(1)}, f32[1152]{0:T(1024)}, u32[]{:S(2)}) copy-start(f32[1152]{0:T(1024)} %param.8) | copy-start | bytes 13828
  161.7 1.7 %copy-start.4 = (bf16[128,1152]{1,0:T(8,128)(2,1)S(1)}, bf16[128,1152]{1,0:T(8,128)(2,1)}, u32[]{:S(2)}) copy-start(bf16[128,1152]{1,0:T(8,128)(2,1)} %param.7) | copy-start | bytes 884740

commit v2 on v1

--- a/solution.py
+++ b/solution.py
@@ -10,6 +10,7 @@
 HEADS = 16
 HEAD = 72
 LANES = 128
+WINDOW = 3
 SCALE = HEAD ** (-0.5)
 MESH = pl.DeviceIdType.MESH
 VMEM = pl.BlockSpec(memory_space=pltpu.VMEM)
@@ -46,8 +47,37 @@
     return far, (me, flip(part, 1)), (me, flip(part, 2)), me
 
 
-def gather_kernel(groups, width, pay, wqkv, wout, qkv, gatt, tracks, held, s_dp, r_dp, s_y, r_y, s_c, r_c):
+def select_heads(width, heads, whole, whole_out, wqkv, wout):
+    first = lax.axis_index("seq") * (heads * HEAD)
+    span = heads * LANES
+    row = lax.broadcasted_iota(jnp.int32, (width, span), 0)
+    column = lax.broadcasted_iota(jnp.int32, (width, span), 1)
+    pick = jnp.zeros((width, span), jnp.bool_)
+    for j in range(heads):
+        inside = (column >= j * LANES) & (column < j * LANES + HEAD)
+        pick = pick | (inside & (row == column + (first + j * (HEAD - LANES))))
+    pick = pick.astype(F32).astype(BF)
+
+    def some_rows(i, carry):
+        rows = pl.ds(pl.multiple_of(i * LANES, LANES), LANES)
+        for j in range(3):
+            wqkv[rows, j * span : (j + 1) * span] = dot(whole[rows, j * width : (j + 1) * width], pick).astype(BF)
+        return carry
+
+    lax.fori_loop(0, width // LANES, some_rows, 0)
+    for j in range(heads):
+        row = lax.broadcasted_iota(jnp.int32, (LANES, width), 0)
+        column = lax.broadcasted_iota(jnp.int32, (LANES, width), 1)
+        pick = ((row < HEAD) & (column == row + (first + j * HEAD))).astype(F32).astype(BF)
+        wout[j * LANES : (j + 1) * LANES, :] = dot(pick, whole_out[...]).astype(BF)
+
+
+def gather_kernel(groups, width, heads, pay, w_qkv, w_out, qkv, gatt, tracks, wqkv, wout, held, whole, whole_out, s_w, s_dp, r_dp, s_y, r_y, s_c, r_c):
     far, sibling, across, me = partners_of(groups)
+    load = pltpu.make_async_copy(w_qkv, whole, s_w.at[0])
+    load_out = pltpu.make_async_copy(w_out, whole_out, s_w.at[1])
+    load.start()
+    load_out.start()
     greet(far[1:] + [sibling, across])
     cap = pay.shape[1]
 
@@ -61,63 +91,88 @@
         for o in range(groups)
     ]
     half = groups // 2
-    for o in list(range(half, groups)) + list(range(1, half)):
+    queue = [half]
+    for o in range(1, half):
+        queue += [o, half + o]
+    order = [0] + queue
+    for o in queue[:WINDOW]:
         first[o].start()
     held[0, 0] = pay[me]
     to_y = [remote(held.at[o, 0], held.at[o, 2], s_y.at[o], r_y.at[o], across) for o in range(groups)]
     to_c = [remote(held.at[o, 0], held.at[o, 1], s_c.at[o, 0], r_c.at[o, 0], sibling) for o in range(groups)]
     to_d = [remote(held.at[o, 2], held.at[o, 3], s_c.at[o, 1], r_c.at[o, 1], sibling) for o in range(groups)]
+    def arrive(step):
+        o = order[step]
+        if step:
+            first[o].wait()
+            if step + WINDOW <= len(queue):
+                first[queue[step + WINDOW - 1]].start()
+        to_y[o].start()
+        to_c[o].start()
+
+    def forward(step):
+        o = order[step]
+        to_y[o].wait_recv()
+        to_d[o].start()
+
+    def project(step):
+        o = order[step]
+        to_c[o].wait_recv()
+        to_d[o].wait_recv()
+        block = held[o].reshape(4 * cap, held.shape[3])
+        rows = pl.ds(o * 4 * cap, 4 * cap)
+        qkv[rows, :] = dot(block[:, :width], wqkv[...]).astype(BF)
+        gatt[rows, :] = dot(block[:, width : 2 * width], wout[...], NT).astype(BF)
+        tracks[rows, :] = block[:, 2 * width :]
+
     for step in range(groups + 2):
         if step < groups:
-            if step:
-                first[step].wait_recv()
-            to_y[step].start()
-            to_c[step].start()
+            arrive(step)
+        if step == 0:
+            load.wait()
+            load_out.wait()
+            select_heads(width, heads, whole, whole_out, wqkv, wout)
         if 1 <= step <= groups:
-            to_y[step - 1].wait_recv()
-            to_d[step - 1].start()
+            forward(step - 1)
         if step >= 2:
-            o = step - 2
-            to_c[o].wait_recv()
-            to_d[o].wait_recv()
-            block = held[o].reshape(4 * cap, held.shape[3])
-            rows = pl.ds(o * 4 * cap, 4 * cap)
-            qkv[rows, :] = dot(block[:, :width], wqkv[...]).astype(BF)
-            gatt[rows, :] = dot(block[:, width : 2 * width], wout[...], NT).astype(BF)
-            tracks[rows, :] = block[:, 2 * width :]
+            project(step - 2)
     for o in range(groups):
-        if o:
-            first[o].wait_send()
         to_y[o].wait_send()
         to_c[o].wait_send()
         to_d[o].wait_send()
 
 
-def gather(pay, wqkv, wout, groups, width):
+def gather(pay, w_qkv, w_out, groups, width, heads):
     cap, columns = pay.shape[1:]
     slots = groups * cap * 4
+    span = heads * LANES
     sems = pltpu.SemaphoreType.DMA
     return pl.pallas_call(
-        functools.partial(gather_kernel, groups, width),
+        functools.partial(gather_kernel, groups, width, heads),
         out_shape=(
-            jax.ShapeDtypeStruct((slots, wqkv.shape[1]), BF),
-            jax.ShapeDtypeStruct((slots, wout.shape[0]), BF),
+            jax.ShapeDtypeStruct((slots, 3 * span), BF),
+            jax.ShapeDtypeStruct((slots, span), BF),
             jax.ShapeDtypeStruct((slots, LANES), BF),
+            jax.ShapeDtypeStruct((width, 3 * span), BF),
+            jax.ShapeDtypeStruct((span, width), BF),
         ),
-        in_specs=[VMEM] * 3,
-        out_specs=(VMEM,) * 3,
+        in_specs=[VMEM, pl.BlockSpec(memory_space=pl.ANY), pl.BlockSpec(memory_space=pl.ANY)],
+        out_specs=(VMEM,) * 5,
         scratch_shapes=[
             pltpu.VMEM((groups, 4, cap, columns), BF),
+            pltpu.VMEM(w_qkv.shape, BF),
+            pltpu.VMEM(w_out.shape, BF),
+            sems((2,)),
             sems((groups,)), sems((groups,)), sems((groups,)), sems((groups,)),
             sems((groups, 2)), sems((groups, 2)),
         ],
         compiler_params=pltpu.CompilerParams(
-            collective_id=0, has_side_effects=True, vmem_limit_bytes=48 * 2**20
+            collective_id=0, has_side_effects=True, vmem_limit_bytes=56 * 2**20
         ),
-    )(pay, wqkv, wout)
-
-
-def scatter_kernel(groups, width, att, dqkv, wqkv, wout, out, part, near, total, passed, crossed, ready, s_dp, r_dp, s_y, r_y, s_c, r_c):
+    )(pay, w_qkv, w_out)
+
+
+def scatter_kernel(groups, width, att, dq, dk, dv, wqkv, wout, out, part, near, total, passed, crossed, ready, s_dp, r_dp, s_y, r_y, s_c, r_c):
     far, sibling, across, me = partners_of(groups)
     greet(far[1:] + [sibling, across])
     cap = out.shape[1]
@@ -142,7 +197,11 @@
     def compute(o):
         rows = pl.ds(o * 4 * cap, 4 * cap)
         part[o, :, :, :width] = dot(att[rows, :], wout[...]).astype(BF).reshape(4, cap, width)
-        part[o, :, :, width:] = dot(dqkv[rows, :], wqkv[...], NT).astype(BF).reshape(4, cap, width)
+        span = att.shape[1]
+        normed = dot(dq[rows, :], wqkv[:, :span], NT)
+        normed += dot(dk[rows, :], wqkv[:, span : 2 * span], NT)
+        normed += dot(dv[rows, :], wqkv[:, 2 * span :], NT)
+        part[o, :, :, width:] = normed.astype(BF).reshape(4, cap, width)
         to_c[o][0].start()
         to_c[o][1].start()
 
@@ -177,7 +236,7 @@
             home[o].wait()
 
 
-def scatter(att, dqkv, wqkv, wout, groups, width):
+def scatter(att, dq, dk, dv, wqkv, wout, groups, width):
     slots = att.shape[0]
     cap = slots // (4 * groups)
     sems = pltpu.SemaphoreType.DMA
@@ -185,7 +244,7 @@
     return pl.pallas_call(
         functools.partial(scatter_kernel, groups, width),
         out_shape=jax.ShapeDtypeStruct((groups, cap, 2 * width), BF),
-        in_specs=[VMEM] * 4,
+        in_specs=[VMEM] * 6,
         out_specs=VMEM,
         scratch_shapes=[
             pltpu.VMEM((groups, 4, cap, 2 * width), BF),
@@ -197,7 +256,7 @@
         compiler_params=pltpu.CompilerParams(
             collective_id=1, has_side_effects=True, vmem_limit_bytes=56 * 2**20
         ),
-    )(att, dqkv, wqkv, wout)
+    )(att, dq, dk, dv, wqkv, wout)
 
 
 def attention_kernel(tiles, query, key, value, grad, tq, tk, att, dq, dk, dv, dk_t, dv_t):
@@ -281,15 +340,14 @@
     payload = jnp.concatenate([normed.astype(BF), cotangent, marks], axis=1)
     payload = dot(placing.astype(BF), payload).astype(BF).reshape(groups, capacity, -1)
 
-    pad = LANES - HEAD
-    mine = lax.dynamic_index_in_dim(w_qkv.reshape(width, 3, parts, heads, HEAD), part, 2, keepdims=False)
-    mine = jnp.pad(mine, ((0, 0), (0, 0), (0, 0), (0, pad))).reshape(width, 3 * heads * LANES)
-    mine_out = lax.dynamic_index_in_dim(w_out.reshape(parts, heads, HEAD, width), part, 0, keepdims=False)
-    mine_out = jnp.pad(mine_out, ((0, 0), (0, pad), (0, 0))).reshape(heads * LANES, width)
-
     if own:
-        qkv, gatt, marked = gather(payload, mine, mine_out, groups, width)
+        qkv, gatt, marked, mine, mine_out = gather(payload, w_qkv, w_out, groups, width, heads)
     else:
+        pad = LANES - HEAD
+        mine = lax.dynamic_index_in_dim(w_qkv.reshape(width, 3, parts, heads, HEAD), part, 2, keepdims=False)
+        mine = jnp.pad(mine, ((0, 0), (0, 0), (0, 0), (0, pad))).reshape(width, 3 * heads * LANES)
+        mine_out = lax.dynamic_index_in_dim(w_out.reshape(parts, heads, HEAD, width), part, 0, keepdims=False)
+        mine_out = jnp.pad(mine_out, ((0, 0), (0, pad), (0, 0))).reshape(heads * LANES, width)
         moved = lax.all_to_all(payload.reshape(slots, -1), "dp", split_axis=0, concat_axis=0, tiled=True)
         moved = lax.all_gather(moved, "seq", axis=0, tiled=True)
         qkv = dot(moved[:, :width], mine).astype(BF)
@@ -297,11 +355,11 @@
         marked = moved[:, 2 * width :]
 
     att, dq, dk, dv = attention(qkv, gatt, marked[:, 0].astype(F32))
-    dqkv = jnp.concatenate([dq, dk, dv], axis=1)
 
     if own:
-        back = scatter(att, dqkv, mine, mine_out, groups, width)
+        back = scatter(att, dq, dk, dv, mine, mine_out, groups, width)
     else:
+        dqkv = jnp.concatenate([dq, dk, dv], axis=1)
         sums = jnp.concatenate([dot(att, mine_out), dot(dqkv, mine, NT)], axis=1).astype(BF)
         sums = lax.all_to_all(sums.reshape(parts, slots, -1), "seq", split_axis=0, concat_axis=0, tiled=True)
         sums = jnp.sum(sums.astype(F32), axis=0).astype(BF)

time: 166 us -> 140 us (0.84)
  local copies, waits for them, and re-layouts: 27.8 us -> 4.04 us
  Pallas kernels: 122 us -> 120 us
    unnamed x15 -> x16, local copies, waits for them, and re-layouts: 16.9 us -> 3.95 us
    pallas_call x1, Pallas kernels: 49.5 us -> 42.5 us  [scatter(): pl.pallas_call(functools.partial(scatter_kernel, groups, width), out_shap...]
    reshape x1 -> x0, local copies, waits for them, and re-layouts: 5.74 us -> none  [local(): jnp.pad(mine, ((0, 0), (0, 0), (0, 0), (0, pad)))]
    pallas_call x1, Pallas kernels: 45.8 us -> 50.3 us  [gather(): pl.pallas_call(functools.partial(gather_kernel, groups, width, heads), ou...]
    pad x2 -> x0, local copies, waits for them, and re-layouts: 3.37 us -> none  [the longest x1 2.27 us: local(): jnp.pad(mine, ((0, 0), (0, 0), (0, 0), (0, pad)))]
    convert_element_type x2, other arithmetic: 0.18 us -> 2.17 us  [local(): att, dq, dk, dv = attention(qkv, gatt, marked[:, 0].astype(F32))]
    concatenate x1 -> x0, other arithmetic: 1.77 us -> none  [local(): dqkv = jnp.concatenate([dq, dk, dv], axis=1)]
    squeeze x2 -> x0, local copies, waits for them, and re-layouts: 1.77 us -> none  [the longest x1 1.71 us: local(): lax.dynamic_index_in_dim(w_qkv.reshape(width, 3, parts, heads, HEAD), par...]
where the time goes in v2:
time: 140 us; the launch traced here: 139 us
  Pallas kernels  120 us (86%)
  other arithmetic  11.4 us (8%)
  local copies, waits for them, and re-layouts  4.04 us (3%)
  matrix products  3.17 us (2%)
    pallas_call x1, Pallas kernels, gather(): pl.pallas_call(functools.partial(gather_kernel, groups, width, heads), ou...  50.3 us
    pallas_call x1, Pallas kernels, scatter(): pl.pallas_call(functools.partial(scatter_kernel, groups, width), out_shap...  42.5 us
    pallas_call x1, Pallas kernels, attention(): pl.pallas_call(functools.partial(attention_kernel, tiles), grid=(heads, t...  27.3 us
    unnamed x16, local copies, waits for them, and re-layouts  3.95 us
    dot_general x2, matrix products, dot(): return lax.dot_general(a, b, dims, preferred_element_type=F32)  3.17 us

profile of v2, /device:TPU:0, one launch (start us, length us, event | category | flops | bytes accessed | tf_op | source)
XLA Modules:
  0.0 139.5 jit_solution(7673243936252965215)
XLA Ops:
  0.6 0.0 copy-start.6
  0.6 0.7 add_convert_fusion.1
  1.3 1.1 convert_reduce_fusion
  2.4 1.2 fusion.9
  3.6 0.1 broadcast_in_dim.6
  3.7 0.7 fusion.18
  4.5 0.2 reduce_window_sum.11
  4.6 0.8 select_reduce_fusion
  5.5 0.7 fusion.19
  6.1 0.7 multiply_add_fusion.1
  6.8 1.2 fusion.11
  8.0 0.0 copy-done.6
  8.0 1.5 %convolution_convert_fusion = bf16[256,2432]{1,0:T(8,128)(2,1)} fusion(bf16[128,128]{1,0:T(8,128)(2,1)S(1)} %broadcast_in_dim.6, bf16[128,1152]{1,0:T(8,128)(2,1)S(1)} %copy-done.6, bf16[128,1152]{1,0:T(8,128)(2,1)S(1)} %fusion.11, s32[128]{0:T(128)S(1)} %multiply_add_fusion.1), kind=kOutput, calls=%fused_computation | convolution fusion | flops 161906688 | bytes 1868288 | tf_op jit(solution)/shard_map/dot_general | solution.py:24
  9.5 50.3 %shard_map.86 = (bf16[1024,1536]{1,0:T(8,128)(2,1)}, bf16[1024,512]{1,0:T(8,128)(2,1)}, bf16[1024,128]{1,0:T(8,128)(2,1)}, bf16[1152,1536]{1,0:T(8,128)(2,1)}, bf16[512,1152]{1,0:T(8,128)(2,1)}) custom-call(bf16[8,32,2432]{2,1,0:T(8,128)(2,1)} %bitcast.13, bf16[1152,3456]{1,0:T(8,128)(2,1)} %w_qkv.1, bf16[1152,1152]{1,0:T(8,128)(2,1)} %w_out.1), custom_call_target="tpu_custom_call" | custom-call | tf_op jit(solution)/shard_map/pallas_call | solution.py:150
  59.8 0.0 copy-start
  59.8 1.2 fusion.15
  61.0 1.0 slice_convert_fusion.tq
  62.0 0.0 copy-done
  62.0 27.3 %shard_map.87 = (bf16[1024,512]{1,0:T(8,128)(2,1)S(1)}, bf16[1024,512]{1,0:T(8,128)(2,1)S(1)}, bf16[1024,512]{1,0:T(8,128)(2,1)S(1)}, bf16[1024,512]{1,0:T(8,128)(2,1)S(1)}) custom-call(bf16[1024,1536]{1,0:T(8,128)(2,1)} %get-tuple-element.11.query.key.value, bf16[1024,1536]{1,0:T(8,128)(2,1)} %get-tuple-element.11.query.key.value, ...), custom_call_target="tpu_custom_call" | custom-call | tf_op jit(solution)/shard_map/pallas_call | solution.py:298
  89.3 0.0 copy-start.1
  89.3 1.0 copy-done.1
  90.3 0.0 copy-start.2
  90.3 1.0 copy-done.2
  91.3 0.0 copy-start.3
  91.3 1.0 copy-done.3
  92.3 0.0 copy-start.4
  92.3 1.0 copy-done.4
  93.2 42.5 %shard_map.88 = bf16[8,32,2304]{2,1,0:T(8,128)(2,1)} custom-call(bf16[1024,512]{1,0:T(8,128)(2,1)} %copy-done.1, bf16[1024,512]{1,0:T(8,128)(2,1)} %copy-done.2, bf16[1024,512]{1,0:T(8,128)(2,1)} %copy-done.3, bf16[1024,512]{1,0:T(8,128)(2,1)} %copy-done.4, bf16[1152,1536]{1,0:T(8,128)(2,1)} %get-tuple-element.18.wqkv, bf16[512,1152]{1,0:T(8,128)(2,1)} %get-tuple-element.19.wout), custom_call_target="tpu_custom_call" | custom-call | tf_op jit(solution)/shard_map/pallas_call | solution.py:244
  135.7 0.0 copy-start.5
  135.7 0.0 copy-start.7
  135.7 1.7 %fusion.14 = f32[128,2304]{1,0:T(8,128)S(1)} fusion(bf16[256,2304]{1,0:T(8,128)(2,1)} %bitcast.14, s32[128]{0:T(128)S(1)} %fusion.19), kind=kOutput, calls=%fused_computation.24 | convolution fusion | flops 151027712 | bytes 2359808 | tf_op jit(solution)/shard_map/dot_general | solution.py:24
  137.4 0.0 copy-done.5
  137.4 0.0 copy-done.7
  137.4 0.2 fusion.12
  137.7 0.9 fusion.22
  138.6 0.9 add_convert_fusion
  (4 shorter events, 0.0 us)
Async XLA Ops:
  0.6 7.4 %copy-start.6 = (bf16[128,1152]{1,0:T(8,128)(2,1)S(1)}, bf16[128,1152]{1,0:T(8,128)(2,1)}, u32[]{:S(2)}) copy-start(bf16[128,1152]{1,0:T(8,128)(2,1)} %param.13) | copy-start | bytes 884740
  59.8 2.2 %copy-start = (bf16[1024,512]{1,0:T(8,128)(2,1)S(1)}, bf16[1024,512]{1,0:T(8,128)(2,1)}, u32[]{:S(2)}) copy-start(bf16[1024,512]{1,0:T(8,128)(2,1)} %get-tuple-element.12.grad) | copy-start | bytes 3145732
  89.3 1.0 copy-start.1
  90.3 1.0 copy-start.2
  91.3 1.0 copy-start.3
  92.3 1.0 copy-start.4
  135.7 1.7 %copy-start.5 = (bf16[128,1152]{1,0:T(8,128)(2,1)S(1)}, bf16[128,1152]{1,0:T(8,128)(2,1)}, u32[]{:S(2)}) copy-start(bf16[128,1152]{1,0:T(8,128)(2,1)} %param.7) | copy-start | bytes 884740
  135.7 1.7 %copy-start.7 = (f32[1152]{0:T(1024)S(1)}, f32[1152]{0:T(1024)}, u32[]{:S(2)}) copy-start(f32[1152]{0:T(1024)} %param.8) | copy-start | bytes 13828

commit v3 on v1

v3 whole, which is shorter than its diff:
```python
import functools

import jax
import jax.numpy as jnp
from jax import lax
from jax.experimental import pallas as pl
from jax.experimental.pallas import tpu as pltpu
from jax.sharding import PartitionSpec as P

HEADS = 16
HEAD = 72
LANES = 128
SCALE = HEAD ** (-0.5)
MESH = pl.DeviceIdType.MESH
VMEM = pl.BlockSpec(memory_space=pltpu.VMEM)
BF = jnp.bfloat16
F32 = jnp.float32
NT = (((1,), (1,)), ((), ()))
TN = (((0,), (0,)), ((), ()))


def dot(a, b, dims=(((1,), (0,)), ((), ()))):
    return lax.dot_general(a, b, dims, preferred_element_type=F32)


def flip(index, mask):
    bit = 1
    out = index
    while bit <= mask:
        if mask & bit:
            out = out + bit * (1 - 2 * ((index // bit) % 2))
        bit *= 2
    return out


def partners_of(groups):
    me, part = lax.axis_index("dp"), lax.axis_index("seq")
    far = [(flip(me, o), part) for o in range(groups)]
    return far, (me, flip(part, 1)), (me, flip(part, 2)), me


def picks(width, heads, first):
    span = heads * LANES
    row = lax.broadcasted_iota(jnp.int32, (width, span), 0)
    column = lax.broadcasted_iota(jnp.int32, (width, span), 1)
    pick = jnp.zeros((width, span), jnp.bool_)
    for j in range(heads):
        inside = (column >= j * LANES) & (column < j * LANES + HEAD)
        pick = pick | (inside & (row == column + (first + j * (HEAD - LANES))))
    return pick.astype(F32).astype(BF)


def remote(src, dst, send, recv, device):
    return pltpu.make_async_remote_copy(
        src_ref=src, dst_ref=dst, send_sem=send, recv_sem=recv, device_id=device, device_id_type=MESH
    )


class Gather:
    def __init__(self, order, places, pay, held, sems):
        far, sibling, across, me = places
        s_dp, r_dp, s_y, r_y, s_c, r_c = sems
        self.order, self.pay, self.held, self.me = order, pay, held, me
        n = len(order)
        self.first = [
            remote(pay.at[far[o][0]], held.at[o, 0], s_dp.at[o], r_dp.at[o], far[o]) if o else None
            for o in range(n)
        ]
        self.to_y = [remote(held.at[o, 0], held.at[o, 2], s_y.at[o], r_y.at[o], across) for o in range(n)]
        self.to_c = [remote(held.at[o, 0], held.at[o, 1], s_c.at[o, 0], r_c.at[o, 0], sibling) for o in range(n)]
        self.to_d = [remote(held.at[o, 2], held.at[o, 3], s_c.at[o, 1], r_c.at[o, 1], sibling) for o in range(n)]

    def send(self, step):
        o = self.order[step]
        if o:
            self.first[o].start()
        else:
            self.held[0, 0] = self.pay[self.me]

    def arrive(self, step):
        o = self.order[step]
        if o:
            self.first[o].wait()
        self.to_y[o].start()
        self.to_c[o].start()

    def forward(self, step):
        o = self.order[step]
        self.to_y[o].wait_recv()
        self.to_d[o].start()

    def ready(self, step):
        o = self.order[step]
        self.to_c[o].wait_recv()
        self.to_d[o].wait_recv()
        return o

    def finish(self):
        for o in range(len(self.order)):
            self.to_y[o].wait_send()
            self.to_c[o].wait_send()
            self.to_d[o].wait_send()


class Scatter:
    def __init__(self, order, places, part, near, total, passed, crossed, home, sems):
        far, sibling, across, _ = places
        s_dp, r_dp, s_y, r_y, s_c, r_c = sems
        self.order, self.part, self.near, self.total = order, part, near, total
        self.passed, self.crossed, self.home = passed, crossed, home
        n = len(order)
        self.to_c = [
            [remote(part.at[o, 2 * j + 1], near.at[o, j], s_c.at[o, j], r_c.at[o, j], sibling) for j in (0, 1)]
            for o in range(n)
        ]
        self.to_y = [remote(passed.at[o], crossed.at[o], s_y.at[o], r_y.at[o], across) for o in range(n)]
        self.to_home = [
            remote(total.at[o], home.at[o], s_dp.at[o], r_dp.at[o], far[o]) if o else None for o in range(n)
        ]

    def put(self, step, value):
        o = self.order[step]
        self.part[o] = value.reshape(self.part.shape[1:])
        self.to_c[o][0].start()
        self.to_c[o][1].start()

    def middle(self, step):
        o = self.order[step]
        self.to_c[o][0].wait_recv()
        self.to_c[o][1].wait_recv()
        self.passed[o] = (self.part[o, 2].astype(F32) + self.near[o, 1].astype(F32)).astype(BF)
        self.to_y[o].start()

    def last(self, step):
        o = self.order[step]
        self.to_y[o].wait_recv()
        value = self.part[o, 0].astype(F32) + self.near[o, 0].astype(F32) + self.crossed[o].astype(F32)
        if o:
            self.total[o] = value.astype(BF)
            self.to_home[o].start()
        else:
            self.home[0] = value.astype(BF)

    def finish(self):
        for o in range(len(self.order)):
            self.to_c[o][0].wait_send()
            self.to_c[o][1].wait_send()
            self.to_y[o].wait_send()
            if o:
                self.to_home[o].wait()


def fused_kernel(groups, heads, tokens, cotangent, gain, dest, track, w_qkv, w_out, output, grad_tokens,
                 pay_a, pay_b, held_a, held_b, whole, whole_out, wqkv, wout, qkv, gatt, att, dqkv,
                 tcol, trow, prob_s, dk_t, dv_t, part_a, part_b, near_a, near_b, total_a, total_b,
                 passed_a, passed_b, crossed_a, crossed_b, home_a, home_b, s_w, *sems):
    count, width = tokens.shape
    cap = pay_a.shape[1]
    slots, rows_all, span = groups * cap, groups * cap * 4, heads * LANES
    block = 4 * cap
    places = partners_of(groups)
    far, sibling, across, me = places
    barrier = pltpu.get_barrier_semaphore()
    greeted = far[1:] + [sibling, across]
    for device in greeted:
        pl.semaphore_signal(barrier, inc=1, device_id=device, device_id_type=MESH)
    load = pltpu.make_async_copy(w_qkv, whole, s_w.at[0])
    load_out = pltpu.make_async_copy(w_out, whole_out, s_w.at[1])
    load.start()
    load_out.start()

    x = tokens[...].astype(F32)
    centred = x - jnp.mean(x, axis=1, keepdims=True)
    scale = lax.rsqrt(jnp.mean(centred * centred, axis=1, keepdims=True) + 1e-06)
    normed = (centred * scale * gain[...]).astype(BF)
    group = dest[...]
    lane = lax.broadcasted_iota(jnp.int32, (count, LANES), 1)
    onehot = (group == lane).astype(F32)
    row = lax.broadcasted_iota(jnp.int32, (count, count), 0)
    column = lax.broadcasted_iota(jnp.int32, (count, count), 1)
    before = dot((column < row).astype(F32).astype(BF), onehot.astype(BF))
    rank = jnp.sum(before * onehot, axis=1, keepdims=True).astype(jnp.int32)
    slot = lax.broadcasted_iota(jnp.int32, (count, slots), 1)
    placing = (group * cap + rank == slot).astype(F32).astype(BF)
    placing_back = ((group ^ me) * cap + rank == slot).astype(F32).astype(BF)
    marks = jnp.broadcast_to((track[...] + 1).astype(F32), (count, LANES)).astype(BF)
    pay_a[:, :, :width] = dot(placing, normed, TN).astype(BF).reshape(groups, cap, width)
    pay_a[:, :, width:] = dot(placing, marks, TN).astype(BF).reshape(groups, cap, LANES)
    pay_b[...] = dot(placing, cotangent[...], TN).astype(BF).reshape(groups, cap, width)
    pl.semaphore_wait(barrier, len(greeted))

    half = groups // 2
    order = [0]
    for i in range(half):
        order += [half + i] + ([i + 1] if i + 1 < half else [])
    a = Gather(order, places, pay_a, held_a, [s.at[0] for s in sems])
    b = Gather(order, places, pay_b, held_b, [s.at[1] for s in sems])
    for step in range(groups):
        a.send(step)

    mine = lax.axis_index("seq") * (heads * HEAD)

    def select(start, stop):
        pick = picks(width, heads, mine)

        def some_rows(i, carry):
            rows = pl.ds(pl.multiple_of(i * LANES, LANES), LANES)
            for j in range(3):
                wqkv[rows, j * span : (j + 1) * span] = dot(whole[rows, j * width : (j + 1) * width], pick).astype(BF)
            return carry

        lax.fori_loop(start, stop, some_rows, 0)

    def project(step):
        o = a.ready(step)
        rows = pl.ds(o * block, block)
        held = held_a[o].reshape(block, width + LANES)
        qkv[rows, :] = dot(held[:, :width], wqkv[...]).astype(BF)
        marked = held[:, width:]
        tcol[rows, :] = marked
        first = (lax.broadcasted_iota(jnp.int32, (8, LANES), 1) == 0).astype(F32).astype(BF)
        trow[:, o * block : (o + 1) * block] = dot(first, marked, NT)

    def project_grad(step):
        o = b.ready(step)
        held = held_b[o].reshape(block, width)
        gatt[o * block : (o + 1) * block, :] = dot(held, wout[...], NT).astype(BF)

    chunks = width // LANES
    for step in range(groups + 3):
        if step < groups:
            a.arrive(step)
            b.send(step)
        if step == 0:
            load.wait()
        if 1 <= step <= groups:
            a.forward(step - 1)
        if step < 3:
            select(chunks * step // 3, chunks * (step + 1) // 3)
        if step >= 3:
            project(step - 3)
    load_out.wait()
    for j in range(heads):
        row = lax.broadcasted_iota(jnp.int32, (LANES, width), 0)
        column = lax.broadcasted_iota(jnp.int32, (LANES, width), 1)
        pick = ((row < HEAD) & (column == row + (mine + j * HEAD))).astype(F32).astype(BF)
        wout[j * LANES : (j + 1) * LANES, :] = dot(pick, whole_out[...]).astype(BF)

    tile = 256

    def head(h, base=0):
        return slice(base * span + h * LANES, base * span + (h + 1) * LANES)

    def attend(h):
        def some(t, carry):
            rows = pl.ds(pl.multiple_of(t * tile, tile), tile)
            match = tcol[rows, 0:1].astype(F32) == trow[0:1, :]
            scores = jnp.where(match, dot(qkv[rows, head(h)], qkv[:, head(h, 1)], NT) * SCALE, -1e30)
            expo = jnp.exp(scores - jnp.max(scores, axis=1, keepdims=True))
            weights = (expo * (1.0 / jnp.sum(expo, axis=1, keepdims=True))).astype(BF)
            prob_s[h, rows, :] = weights
            att[rows, head(h)] = dot(weights, qkv[:, head(h, 2)]).astype(BF)
            return carry

        lax.fori_loop(0, rows_all // tile, some, 0)

    def attend_back(h):
        dk_t[...] = jnp.zeros_like(dk_t)
        dv_t[...] = jnp.zeros_like(dv_t)

        def some(t, carry):
            rows = pl.ds(pl.multiple_of(t * tile, tile), tile)
            weights = prob_s[h, rows, :]
            g = gatt[rows, head(h)]
            delta = jnp.sum(g.astype(F32) * att[rows, head(h)].astype(F32), axis=1, keepdims=True)
            dscore = (weights.astype(F32) * (dot(g, qkv[:, head(h, 2)], NT) - delta)).astype(BF)
            dqkv[rows, head(h)] = (dot(dscore, qkv[:, head(h, 1)]) * SCALE).astype(BF)
            dk_t[...] += dot(qkv[rows, head(h)], dscore, TN)
            dv_t[...] += dot(g, weights, TN)
            return carry

        lax.fori_loop(0, rows_all // tile, some, 0)
        dqkv[:, head(h, 1)] = (dk_t[...].T * SCALE).astype(BF)
        dqkv[:, head(h, 2)] = dv_t[...].T.astype(BF)

    each = groups // heads
    for h in range(heads):
        for step in range(each * h, each * (h + 1)):
            b.arrive(step)
        for step in range(each * (h - 1), each * h):
            if step >= 0:
                b.forward(step)
        attend(h)
    for step in range(each * (heads - 1), groups):
        b.forward(step)

    home_order = list(range(half, groups)) + list(range(1, half)) + [0]
    out_a = Scatter(home_order, places, part_a, near_a, total_a, passed_a, crossed_a, home_a, [s.at[2] for s in sems])
    out_b = Scatter(home_order, places, part_b, near_b, total_b, passed_b, crossed_b, home_b, [s.at[3] for s in sems])
    for step in range(groups):
        o = home_order[step]
        out_a.put(step, dot(att[o * block : (o + 1) * block, :], wout[...]).astype(BF))
        if step:
            out_a.middle(step - 1)
    out_a.middle(groups - 1)
    for step in range(groups):
        project_grad(step)

    done = 0
    for h in range(heads):
        attend_back(h)
        until = min(groups, (h + 1) * ((groups + 2) // 3))
        for step in range(done, until):
            out_a.last(step)
        done = until
    for step in range(groups + 2):
        if step < groups:
            o = home_order[step]
            out_b.put(step, dot(dqkv[o * block : (o + 1) * block, :], wqkv[...], NT).astype(BF))
        if 1 <= step <= groups:
            out_b.middle(step - 1)
        if step >= 2:
            out_b.last(step - 2)
    a.finish()
    b.finish()
    out_a.finish()
    back = dot(placing_back, home_a[...].reshape(slots, width))
    output[...] = (tokens[...].astype(F32) + back).astype(BF)
    out_b.finish()
    back = dot(placing_back, home_b[...].reshape(slots, width)) * gain[...]
    x = tokens[...].astype(F32)
    unit = (x - jnp.mean(x, axis=1, keepdims=True)) * scale
    back = back - jnp.mean(back, axis=1, keepdims=True) - unit * jnp.mean(back * unit, axis=1, keepdims=True)
    grad_tokens[...] = (cotangent[...].astype(F32) + scale * back).astype(BF)


def fused(tokens, gain, w_qkv, w_out, dest, track, cotangent, groups, heads):
    count, width = tokens.shape
    cap = 2 * count // groups
    rows, span = groups * cap * 4, heads * LANES
    sems = pltpu.SemaphoreType.DMA
    buf = lambda *shape: pltpu.VMEM(shape, BF)
    out = jax.ShapeDtypeStruct((count, width), BF)
    anywhere = pl.BlockSpec(memory_space=pl.ANY)
    return pl.pallas_call(
        functools.partial(fused_kernel, groups, heads),
        out_shape=(out, out),
        in_specs=[VMEM] * 5 + [anywhere] * 2,
        out_specs=(VMEM, VMEM),
        scratch_shapes=[
            buf(groups, cap, width + LANES), buf(groups, cap, width),
            buf(groups, 4, cap, width + LANES), buf(groups, 4, cap, width),
            buf(*w_qkv.shape), buf(*w_out.shape),
            buf(width, 3 * span), buf(span, width),
            buf(rows, 3 * span), buf(rows, span), buf(rows, span), buf(rows, 3 * span),
            buf(rows, LANES), pltpu.VMEM((8, rows), F32),
            buf(heads, rows, rows),
            pltpu.VMEM((LANES, rows), F32), pltpu.VMEM((LANES, rows), F32),
            buf(groups, 4, cap, width), buf(groups, 4, cap, width),
            buf(groups, 2, cap, width), buf(groups, 2, cap, width),
        ]
        + [buf(groups, cap, width)] * 8
        + [sems((2,))]
        + [sems((4, groups))] * 4
        + [sems((4, groups, 2))] * 2,
        compiler_params=pltpu.CompilerParams(
            collective_id=0, has_side_effects=True, vmem_limit_bytes=62 * 2**20
        ),
    )(tokens, cotangent, gain[None, :], dest, track[:, None], w_qkv, w_out)


def attention_kernel(tiles, query, key, value, grad, tq, tk, att, dq, dk, dv, dk_t, dv_t):
    tile = pl.program_id(1)
    q, k, v, g = query[...], key[...], value[...], grad[...]
    scores = jnp.where(tq[...] == tk[...], dot(q, k, NT) * SCALE, -1e30)
    top = jnp.max(scores, axis=1, keepdims=True)
    expo = jnp.exp(scores - top)
    prob = expo * (1.0 / jnp.sum(expo, axis=1, keepdims=True))
    weights = prob.astype(BF)
    result = dot(weights, v).astype(BF)
    att[...] = result
    delta = jnp.sum(g.astype(F32) * result.astype(F32), axis=1, keepdims=True)
    dscore = (prob * (dot(g, v, NT) - delta)).astype(BF)
    dq[...] = (dot(dscore, k) * SCALE).astype(BF)

    @pl.when(tile == 0)
    def _():
        dk_t[...] = jnp.zeros_like(dk_t)
        dv_t[...] = jnp.zeros_like(dv_t)

    dk_t[...] += dot(q, dscore, TN)
    dv_t[...] += dot(g, weights, TN)

    @pl.when(tile == tiles - 1)
    def _():
        dk[...] = (dk_t[...].T * SCALE).astype(BF)
        dv[...] = dv_t[...].T.astype(BF)


def attention(qkv, gatt, track):
    slots = qkv.shape[0]
    heads = gatt.shape[1] // LANES
    rows = min(256, slots)
    tiles = slots // rows
    whole = lambda first: pl.BlockSpec((slots, LANES), lambda h, t: (0, first + h))
    part = pl.BlockSpec((rows, LANES), lambda h, t: (t, h))
    out = jax.ShapeDtypeStruct((slots, heads * LANES), BF)
    return pl.pallas_call(
        functools.partial(attention_kernel, tiles),
        grid=(heads, tiles),
        out_shape=(out,) * 4,
        in_specs=[
            part, whole(heads), whole(2 * heads), part,
            pl.BlockSpec((rows, 1), lambda h, t: (t, 0)),
            pl.BlockSpec((1, slots), lambda h, t: (0, 0)),
        ],
        out_specs=(part, part, whole(0), whole(0)),
        scratch_shapes=[pltpu.VMEM((LANES, slots), F32), pltpu.VMEM((LANES, slots), F32)],
        compiler_params=pltpu.CompilerParams(vmem_limit_bytes=48 * 2**20),
    )(qkv, qkv, qkv, gatt, track[:, None], track[None, :])


def normalize(rows, gain):
    mean = jnp.mean(rows, axis=1, keepdims=True)
    centred = rows - mean
    var = jnp.mean(centred * centred, axis=1, keepdims=True)
    return centred * lax.rsqrt(var + 1e-06) * gain[None, :]


def local(tokens, gain, w_qkv, w_out, dest, track, cotangent):
    count, width = tokens.shape
    groups, parts = lax.axis_size("dp"), lax.axis_size("seq")
    capacity = 2 * count // groups
    slots = groups * capacity
    heads = HEADS // parts
    part = lax.axis_index("seq")
    if capacity % 16 == 0 and parts == 4 and groups <= LANES:
        return fused(tokens, gain, w_qkv, w_out, dest, track, cotangent, groups, heads)

    clip_group = dest[:, 0]
    onehot = (clip_group[:, None] == jnp.arange(groups, dtype=jnp.int32)[None, :]).astype(jnp.int32)
    rank = jnp.sum(jnp.cumsum(onehot, axis=0) * onehot, axis=1) - 1
    slot_ids = jnp.arange(slots, dtype=jnp.int32)
    placing = (clip_group * capacity + rank)[None, :] == slot_ids[:, None]
    placing_back = (clip_group * capacity + rank)[:, None] == slot_ids[None, :]

    rows_f = tokens.astype(F32)
    normed, ln_back = jax.vjp(lambda value: normalize(value, gain), rows_f)
    marks = jnp.broadcast_to((track + 1).astype(BF)[:, None], (count, LANES))
    payload = jnp.concatenate([normed.astype(BF), cotangent, marks], axis=1)
    payload = dot(placing.astype(BF), payload).astype(BF).reshape(groups, capacity, -1)

    pad = LANES - HEAD
    mine = lax.dynamic_index_in_dim(w_qkv.reshape(width, 3, parts, heads, HEAD), part, 2, keepdims=False)
    mine = jnp.pad(mine, ((0, 0), (0, 0), (0, 0), (0, pad))).reshape(width, 3 * heads * LANES)
    mine_out = lax.dynamic_index_in_dim(w_out.reshape(parts, heads, HEAD, width), part, 0, keepdims=False)
    mine_out = jnp.pad(mine_out, ((0, 0), (0, pad), (0, 0))).reshape(heads * LANES, width)
    moved = lax.all_to_all(payload.reshape(slots, -1), "dp", split_axis=0, concat_axis=0, tiled=True)
    moved = lax.all_gather(moved, "seq", axis=0, tiled=True)
    qkv = dot(moved[:, :width], mine).astype(BF)
    gatt = dot(moved[:, width : 2 * width], mine_out, NT).astype(BF)
    marked = moved[:, 2 * width :]

    att, dq, dk, dv = attention(qkv, gatt, marked[:, 0].astype(F32))

    dqkv = jnp.concatenate([dq, dk, dv], axis=1)
    sums = jnp.concatenate([dot(att, mine_out), dot(dqkv, mine, NT)], axis=1).astype(BF)
    sums = lax.all_to_all(sums.reshape(parts, slots, -1), "seq", split_axis=0, concat_axis=0, tiled=True)
    sums = jnp.sum(sums.astype(F32), axis=0).astype(BF)
    back = lax.all_to_all(sums, "dp", split_axis=0, concat_axis=0, tiled=True)

    back = dot(placing_back.astype(BF), back.reshape(slots, 2 * width))
    output = (rows_f + back[:, :width]).astype(BF)
    grad_tokens = (cotangent.astype(F32) + ln_back(back[:, width:])[0]).astype(BF)
    return (output, grad_tokens)


def solution(mesh):
    return jax.shard_map(
        local,
        mesh=mesh,
        in_specs=(
            P(("dp", "seq"), None),
            P(),
            P(),
            P(),
            P(("dp", "seq"), None),
            P(("dp", "seq")),
            P(("dp", "seq"), None),
        ),
        out_specs=(P(("dp", "seq"), None), P(("dp", "seq"), None)),
        check_vma=False,
    )
```

time: 166 us -> 111 us (0.67)
  local copies, waits for them, and re-layouts: 27.8 us -> 7.46 us
  Pallas kernels: 122 us -> 103 us
  other arithmetic: 11.2 us -> 0 us
  matrix products: 3.3 us -> 0 us
    pallas_call x3 -> x1, Pallas kernels: 122 us -> 103 us  [fused(): pl.pallas_call(functools.partial(fused_kernel, groups, heads), out_shape=...]
    unnamed x15 -> x3, local copies, waits for them, and re-layouts: 16.9 us -> 4.78 us
    reshape x1 -> x0, local copies, waits for them, and re-layouts: 5.74 us -> none  [local(): jnp.pad(mine, ((0, 0), (0, 0), (0, 0), (0, pad)))]
    reduce_sum x5 -> x0, other arithmetic: 4.27 us -> none  [the longest x1 1.19 us: normalize(): var = jnp.mean(centred * centred, axis=1, keepdims=True)]
    convert_element_type x6 -> x0, other arithmetic: 3.61 us -> none  [the longest x1 1.17 us: local(): payload = jnp.concatenate([normed.astype(BF), cotangent, marks], axis=1)]
    pad x2 -> x0, local copies, waits for them, and re-layouts: 3.37 us -> none  [the longest x1 2.27 us: local(): jnp.pad(mine, ((0, 0), (0, 0), (0, 0), (0, pad)))]
    dot_general x2 -> x0, matrix products: 3.3 us -> none  [dot(): return lax.dot_general(a, b, dims, preferred_element_type=F32)]
    broadcast_in_dim x1 -> x2, local copies, waits for them, and re-layouts: 0.09 us -> 2.68 us  [the longest x1 1.39 us: fused(): track[:, None]]
where the time goes in v3:
time: 111 us
  Pallas kernels  103 us (93%)
  local copies, waits for them, and re-layouts  7.46 us (7%)
    pallas_call x1, Pallas kernels, fused(): pl.pallas_call(functools.partial(fused_kernel, groups, heads), out_shape=...  103 us
    unnamed x3, local copies, waits for them, and re-layouts  4.78 us

profile of v3, /device:TPU:0, one launch (start us, length us, event | category | flops | bytes accessed | tf_op | source)
XLA Modules:
  0.0 110.9 jit_solution(11664188865185902909)
XLA Ops:
  0.6 1.3 %broadcast_in_dim.6.gain = f32[1,1152]{1,0:T(1,128)} reshape(f32[1152]{0:T(1024)} %param.8) | data formatting | bytes 9216 | tf_op jit(solution)/shard_map/broadcast_in_dim | solution.py:369
  1.9 1.4 %copy.9.dest = s32[128,1]{1,0:T(8,128)} copy(s32[128,1]{0,1:T(1,128)} %param.11) | data formatting | bytes 1024 | tf_op args[4]
  3.3 1.4 %copy.10.track = s32[128,1]{1,0:T(8,128)} copy(s32[128,1]{0,1:T(1,128)} %bitcast.1) | data formatting | bytes 1024 | tf_op jit(solution)/shard_map/broadcast_in_dim | solution.py:369
  4.7 102.8 %shard_map.86 = (bf16[128,1152]{1,0:T(8,128)(2,1)}, bf16[128,1152]{1,0:T(8,128)(2,1)}) custom-call(bf16[128,1152]{1,0:T(8,128)(2,1)} %tokens.1, bf16[128,1152]{1,0:T(8,128)(2,1)} %cotangent.1, f32[1,1152]{1,0:T(1,128)} %broadcast_in_dim.6.gain, s32[128,1]{1,0:T(8,128)} %copy.9.dest, s32[128,1]{1,0:T(8,128)} %copy.10.track, bf16[1152,3456]{1,0:T(8,128)(2,1)} %w_qkv.1, ...), custom_call_target="tpu_custom_call" | custom-call | tf_op jit(solution)/shard_map/pallas_call | solution.py:345
  107.5 1.7 %copy.13 = bf16[128,1152]{1,0:T(8,128)(2,1)} copy(bf16[128,1152]{1,0:T(8,128)(2,1)} %get-tuple-element.4) | data formatting | bytes 589824
  109.2 1.7 %copy.14 = bf16[128,1152]{1,0:T(8,128)(2,1)} copy(bf16[128,1152]{1,0:T(8,128)(2,1)} %get-tuple-element.5) | data formatting | bytes 589824

commit v4 on v3

--- a/solution.py
+++ b/solution.py
@@ -173,26 +173,27 @@
     centred = x - jnp.mean(x, axis=1, keepdims=True)
     scale = lax.rsqrt(jnp.mean(centred * centred, axis=1, keepdims=True) + 1e-06)
     normed = (centred * scale * gain[...]).astype(BF)
-    group = dest[...]
+    row = lax.broadcasted_iota(jnp.int32, (count, count), 0)
+    column = lax.broadcasted_iota(jnp.int32, (count, count), 1)
+    upright = lambda line: jnp.sum(jnp.where(row == column, line, 0), axis=1, keepdims=True)
+    group = upright(dest[...])
     lane = lax.broadcasted_iota(jnp.int32, (count, LANES), 1)
     onehot = (group == lane).astype(F32)
-    row = lax.broadcasted_iota(jnp.int32, (count, count), 0)
-    column = lax.broadcasted_iota(jnp.int32, (count, count), 1)
     before = dot((column < row).astype(F32).astype(BF), onehot.astype(BF))
     rank = jnp.sum(before * onehot, axis=1, keepdims=True).astype(jnp.int32)
     slot = lax.broadcasted_iota(jnp.int32, (count, slots), 1)
     placing = (group * cap + rank == slot).astype(F32).astype(BF)
     placing_back = ((group ^ me) * cap + rank == slot).astype(F32).astype(BF)
-    marks = jnp.broadcast_to((track[...] + 1).astype(F32), (count, LANES)).astype(BF)
+    marks = jnp.broadcast_to((upright(track[...]) + 1).astype(F32), (count, LANES)).astype(BF)
     pay_a[:, :, :width] = dot(placing, normed, TN).astype(BF).reshape(groups, cap, width)
     pay_a[:, :, width:] = dot(placing, marks, TN).astype(BF).reshape(groups, cap, LANES)
     pay_b[...] = dot(placing, cotangent[...], TN).astype(BF).reshape(groups, cap, width)
     pl.semaphore_wait(barrier, len(greeted))
 
     half = groups // 2
-    order = [0]
-    for i in range(half):
-        order += [half + i] + ([i + 1] if i + 1 < half else [])
+    order = []
+    for i in range(0, half, 2):
+        order += [i, i + 1, half + i, half + i + 1]
     a = Gather(order, places, pay_a, held_a, [s.at[0] for s in sems])
     b = Gather(order, places, pay_b, held_b, [s.at[1] for s in sems])
     for step in range(groups):
@@ -213,18 +214,20 @@
 
     def project(step):
         o = a.ready(step)
-        rows = pl.ds(o * block, block)
-        held = held_a[o].reshape(block, width + LANES)
+        a.ready(step + 1)
+        rows = slice(o * block, (o + 2) * block)
+        held = held_a[o : o + 2].reshape(2 * block, width + LANES)
         qkv[rows, :] = dot(held[:, :width], wqkv[...]).astype(BF)
         marked = held[:, width:]
         tcol[rows, :] = marked
         first = (lax.broadcasted_iota(jnp.int32, (8, LANES), 1) == 0).astype(F32).astype(BF)
-        trow[:, o * block : (o + 1) * block] = dot(first, marked, NT)
+        trow[:, rows] = dot(first, marked, NT)
 
     def project_grad(step):
         o = b.ready(step)
-        held = held_b[o].reshape(block, width)
-        gatt[o * block : (o + 1) * block, :] = dot(held, wout[...], NT).astype(BF)
+        b.ready(step + 1)
+        held = held_b[o : o + 2].reshape(2 * block, width)
+        gatt[o * block : (o + 2) * block, :] = dot(held, wout[...], NT).astype(BF)
 
     chunks = width // LANES
     for step in range(groups + 3):
@@ -237,8 +240,8 @@
             a.forward(step - 1)
         if step < 3:
             select(chunks * step // 3, chunks * (step + 1) // 3)
-        if step >= 3:
-            project(step - 3)
+        if step >= 3 and step % 2 == 0:
+            project(step - 4)
     load_out.wait()
     for j in range(heads):
         row = lax.broadcasted_iota(jnp.int32, (LANES, width), 0)
@@ -294,16 +297,27 @@
     for step in range(each * (heads - 1), groups):
         b.forward(step)
 
-    home_order = list(range(half, groups)) + list(range(1, half)) + [0]
+    home_order = list(range(half, groups))
+    for i in range(half - 2, 0, -2):
+        home_order += [i, i + 1]
+    home_order += [1, 0]
     out_a = Scatter(home_order, places, part_a, near_a, total_a, passed_a, crossed_a, home_a, [s.at[2] for s in sems])
     out_b = Scatter(home_order, places, part_b, near_b, total_b, passed_b, crossed_b, home_b, [s.at[3] for s in sems])
+
+    def put_two(out, step, left, right, dims):
+        base = min(home_order[step : step + 2])
+        value = dot(left[base * block : (base + 2) * block, :], right[...], dims).astype(BF)
+        for i in (step, step + 1):
+            at = (home_order[i] - base) * block
+            out.put(i, value[at : at + block])
+
     for step in range(groups):
-        o = home_order[step]
-        out_a.put(step, dot(att[o * block : (o + 1) * block, :], wout[...]).astype(BF))
+        if step % 2 == 0:
+            put_two(out_a, step, att, wout, (((1,), (0,)), ((), ())))
         if step:
             out_a.middle(step - 1)
     out_a.middle(groups - 1)
-    for step in range(groups):
+    for step in range(0, groups, 2):
         project_grad(step)
 
     done = 0
@@ -314,9 +328,8 @@
             out_a.last(step)
         done = until
     for step in range(groups + 2):
-        if step < groups:
-            o = home_order[step]
-            out_b.put(step, dot(dqkv[o * block : (o + 1) * block, :], wqkv[...], NT).astype(BF))
+        if step < groups and step % 2 == 0:
+            put_two(out_b, step, dqkv, wqkv, NT)
         if 1 <= step <= groups:
             out_b.middle(step - 1)
         if step >= 2:
@@ -366,7 +379,7 @@
         compiler_params=pltpu.CompilerParams(
             collective_id=0, has_side_effects=True, vmem_limit_bytes=62 * 2**20
         ),
-    )(tokens, cotangent, gain[None, :], dest, track[:, None], w_qkv, w_out)
+    )(tokens, cotangent, gain.reshape(1, width), dest.reshape(1, count), track.reshape(1, count), w_qkv, w_out)
 
 
 def attention_kernel(tiles, query, key, value, grad, tq, tk, att, dq, dk, dv, dk_t, dv_t):

time: 111 us -> 104 us (0.937)
  Pallas kernels: 103 us -> 98 us
  local copies, waits for them, and re-layouts: 7.46 us -> 4.69 us
    pallas_call x1, Pallas kernels: 103 us -> 98 us  [fused(): pl.pallas_call(functools.partial(fused_kernel, groups, heads), out_shape=...]
    broadcast_in_dim x2 -> x0, local copies, waits for them, and re-layouts: 2.68 us -> none  [the longest x1 1.39 us: fused(): track[:, None]]
    unnamed x3 -> x2, local copies, waits for them, and re-layouts: 4.78 us -> 3.4 us
    reshape x0 -> x1, local copies, waits for them, and re-layouts: none -> 1.29 us  [fused(): gain.reshape(1, width)]
where the time goes in v4:
time: 104 us; the launch traced here: 103 us
  Pallas kernels  98 us (94%)
  local copies, waits for them, and re-layouts  4.69 us (5%)
    pallas_call x1, Pallas kernels, fused(): pl.pallas_call(functools.partial(fused_kernel, groups, heads), out_shape=...  98 us
    unnamed x2, local copies, waits for them, and re-layouts  3.4 us

profile of v4, /device:TPU:0, one launch (start us, length us, event | category | flops | bytes accessed | tf_op | source)
XLA Modules:
  0.0 103.3 jit_solution(13849339537904606230)
XLA Ops:
  0.6 1.3 %reshape.13.gain = f32[1,1152]{1,0:T(1,128)} reshape(f32[1152]{0:T(1024)} %param.8) | data formatting | bytes 9216 | tf_op jit(solution)/shard_map/reshape | solution.py:382
  1.9 98.0 %shard_map.86 = (bf16[128,1152]{1,0:T(8,128)(2,1)}, bf16[128,1152]{1,0:T(8,128)(2,1)}) custom-call(bf16[128,1152]{1,0:T(8,128)(2,1)} %tokens.1, bf16[128,1152]{1,0:T(8,128)(2,1)} %cotangent.1, f32[1,1152]{1,0:T(1,128)} %reshape.13.gain, s32[1,128]{1,0:T(1,128)} %bitcast.2, s32[1,128]{1,0:T(1,128)} %bitcast.3, bf16[1152,3456]{1,0:T(8,128)(2,1)} %w_qkv.1, ...), custom_call_target="tpu_custom_call" | custom-call | tf_op jit(solution)/shard_map/pallas_call | solution.py:358
  99.9 1.7 %copy.11 = bf16[128,1152]{1,0:T(8,128)(2,1)} copy(bf16[128,1152]{1,0:T(8,128)(2,1)} %get-tuple-element.4) | data formatting | bytes 589824
  101.6 1.7 %copy.12 = bf16[128,1152]{1,0:T(8,128)(2,1)} copy(bf16[128,1152]{1,0:T(8,128)(2,1)} %get-tuple-element.5) | data formatting | bytes 589824
